TPU v7x, 512 devices: a whole 4x4x16 slice. The times are simulated.
512 devices in a mesh: ry: 32 (over z, y_hi), rx: 16 (over y_lo, x, core).
Axes of the slice: x: 4, y: 4 (y_hi: 2, y_lo: 2; y = y_hi * 2 + y_lo), z: 16, core: 2. Of those that a mesh axis runs over, the one named last changes fastest.
Arguments:
- control: bfloat16 [2, 64, 256, 2048], P(None, None, 'ry', 'rx'), may hold values from -6 to 6
- forcing: bfloat16 [2, 64, 256, 2048], P(None, None, 'ry', 'rx'), may hold values from -0.1796875 to 0.1796875
- obs_tile: int32 [524288, 1], P(('ry', 'rx')), may hold values from 0 to 15; in each aligned block of 1024 rows (0 to 1023, 1024 to 2047, ...) at most 256 rows name the same one
- obs_cell: int32 [524288], P(('ry', 'rx')), may hold values from 0 to 65535
- obs_value: float32 [2, 524288], P(None, ('ry', 'rx')), may hold values from -6 to 6
- obs_count: int32 [512], P(('ry', 'rx')), may hold values from 256 to 1024, as said below
- rate_x: float32 [2048], replicated, may hold values from 0.5 to 8
- rate_y: float32 [256], P('ry'), may hold values from 0.5 to 8
- vert: bfloat16 [2, 64, 64], replicated, may hold values from -0.75 to 0.75
Outputs:
- gradient: bfloat16 [2, 64, 256, 2048], P(None, None, 'ry', 'rx')
Inputs may be any that keep to these rules, and one draw needn't show every extreme that they name: `obs_tile`: among the 1024 slots of one region no tile is named more than 256 times; in some region some tile is named exactly 256 times. `obs_count`: some region uses all 1024 slots.
All inputs are finite; a program needn't handle non-finite values.
Results may differ from a plain program's by a relative error of at most 0.0067.
Values may be sent and summed in bfloat16 or wider, within the bound.
No kernel may reach another device: no remote copies, remote signals or barrier semaphores. Data moves between devices by JAX's collectives and lax.ppermute only.
A program may use at most 192 MiB of HBM per device.

v0:
```python
import jax
import jax.numpy as jnp
from jax import lax
from jax.sharding import PartitionSpec as P

HX = 128
HY = 8


def padded_2(cells, sides, width):
    for axis, dim in sides:
        count = lax.axis_size(axis)
        ends = count - 1
        head = lax.slice_in_dim(cells, 0, width, axis=dim)
        tail = lax.slice_in_dim(cells, cells.shape[dim] - width, cells.shape[dim], axis=dim)
        cells = jnp.concatenate(
            [
                lax.ppermute(tail, axis, [(i, (i + 1) % count) for i in range(ends)]),
                cells,
                lax.ppermute(head, axis, [((i + 1) % count, i) for i in range(ends)]),
            ],
            axis=dim,
        )
    return cells


def band_kernel(rates, reach_cells):
    block_count = rates.shape[0] // reach_cells
    offsets = jnp.arange(3)[:, None, None, None]
    in_cell = jnp.arange(reach_cells)[None, None, :, None]
    out_cell = jnp.arange(reach_cells)[None, None, None, :]
    distance = jnp.abs((offsets - 1) * reach_cells + in_cell - out_cell).astype(jnp.float32)
    scaled = rates.reshape(1, block_count, 1, reach_cells)
    weight = jnp.where(distance <= reach_cells, jnp.exp(-distance * scaled / reach_cells), 0.0)
    return weight.astype(jnp.bfloat16)


def lat_kernel(rates, reach_cells):
    row_count = rates.shape[0]
    out_row = jnp.arange(row_count)[:, None]
    in_row = jnp.arange(row_count + 2 * reach_cells)[None, :]
    distance = jnp.abs(in_row - reach_cells - out_row).astype(jnp.float32)
    weight = jnp.where(
        distance <= reach_cells, jnp.exp(-distance * rates[:, None] / reach_cells), 0.0
    )
    return weight.astype(jnp.bfloat16)


def along_x(padded, kernel):
    block_count = kernel.shape[1]
    reach_cells = kernel.shape[2]
    leading = padded.shape[:-1]
    blocks = padded.reshape(leading + (block_count + 2, reach_cells))
    summed = jnp.zeros(leading + (block_count, reach_cells), jnp.float32)
    for block_shift in range(3):
        summed = summed + jnp.einsum(
            "abcnp,npq->abcnq",
            blocks[:, :, :, block_shift : block_shift + block_count, :],
            kernel[block_shift],
            preferred_element_type=jnp.float32,
        )
    return summed.reshape(leading + (block_count * reach_cells,))


def lat_filter(lat_padded, lat_weights):
    return jnp.einsum(
        "yp,clpx->clyx", lat_weights, lat_padded, preferred_element_type=jnp.float32
    ).astype(jnp.bfloat16)


def body(control, forcing, obs_tile, obs_cell, obs_value, obs_count, rate_x, rate_y, vert):
    components, levels, lat_rows, lon_cols = control.shape
    tile_ids = obs_tile[:, 0]
    slot_total = tile_ids.shape[0]
    usable = jnp.arange(slot_total) < obs_count[0]
    tagged = jnp.where(usable, tile_ids, -1)
    places = jnp.stack([tagged, obs_cell])
    got_places, got_values = (
        lax.all_gather(places, "rx", axis=1, tiled=True),
        lax.all_gather(obs_value, "rx", axis=1, tiled=True),
    )
    mine = got_places[0] == lax.axis_index("rx")
    cell_ids = got_places[1]
    values = jnp.where(mine[None, :], got_values, 0.0)
    base = forcing.astype(jnp.float32).reshape(components, levels * lat_rows * lon_cols)
    scatter_field = base.at[:, cell_ids].add(values)
    observed = scatter_field.astype(jnp.bfloat16).reshape(components, levels, lat_rows, lon_cols)
    lat_weights = lat_kernel(rate_y, HY)
    kernel_all = band_kernel(rate_x, HX)
    padded = jnp.pad(
        lax.all_to_all(observed, "rx", split_axis=1, concat_axis=3, tiled=True),
        ((0, 0), (0, 0), (0, 0), (HX, HX)),
    )
    lon_smooth = along_x(padded, kernel_all).astype(jnp.bfloat16)
    lat_padded = padded_2(lon_smooth, (("ry", 2),), HY)
    lat_smooth = lat_filter(lat_padded, lat_weights)
    columns = jnp.einsum(
        "clm,cmyx->clyx",
        vert,
        lax.all_to_all(lat_smooth, "rx", split_axis=3, concat_axis=1, tiled=True),
        preferred_element_type=jnp.float32,
    )
    return (control.astype(jnp.float32) + columns).astype(jnp.bfloat16)


def solution(mesh):
    placed = (
        P(None, None, "ry", "rx"),
        P(None, None, "ry", "rx"),
        P(("ry", "rx"), None),
        P(("ry", "rx")),
        P(None, ("ry", "rx")),
        P(("ry", "rx")),
        P(),
        P("ry"),
        P(),
    )
    return jax.shard_map(
        body, mesh=mesh, in_specs=placed, out_specs=P(None, None, "ry", "rx"), check_vma=False
    )
```

profile of v0, /device:TPU:24, one launch (start us, length us, event | category | flops | bytes accessed | tf_op | source)
XLA Modules:
  0.0 252.9 jit_solution(13688149622953682249)
XLA Ops:
  0.0 0.0 copy-start
  0.7 0.7 compare_select_fusion.1
  1.4 0.7 pad_add_fusion
  2.1 19.2 %all_gather.6 = s32[2,16384]{1,0:T(2,128)S(1)} all-gather(s32[2,1024]{1,0:T(2,128)S(1)} %pad_add_fusion), channel_id=1, replica_groups=mesh['ry'=32,'rx'=16] {'rx'}, dimensions={1}, use_global_device_ids=true | all-gather | bytes 139264 | tf_op jit(solution)/shard_map/all_gather | solution.py:79
  21.3 0.1 compare_select_fusion
  21.4 0.2 compare_reduce_fusion
  21.6 16.9 %all_gather.7 = f32[2,16384]{1,0:T(2,128)S(1)} all-gather(f32[2,1024]{1,0:T(2,128)} %param.13), channel_id=1, replica_groups=mesh['ry'=32,'rx'=16] {'rx'}, dimensions={1}, use_global_device_ids=true | all-gather | bytes 139264 | tf_op jit(solution)/shard_map/all_gather | solution.py:80
  38.4 0.1 select_bitcast_fusion
  38.5 0.0 copy-start.1
  38.5 4.9 %copy.37 = f32[16384,2]{1,0:T(8,128)} copy(f32[16384,2]{0,1:T(2,128)S(1)} %select_bitcast_fusion) | data formatting | bytes 262144 | tf_op jit(solution)/shard_map/jit(_where)/select_n | solution.py:84
  43.4 0.0 copy-done.1
  43.4 13.9 %copy.36 = f32[2,64,8,128]{0,3,2,1:T(8,128)} copy(bf16[2,64,8,128]{3,2,1,0:T(8,128)(2,1)S(1)} %copy-done.1) | data formatting | bytes 786432 | tf_op jit(solution)/shard_map/reshape | solution.py:85
  57.4 100.3 %scatter_fusion = f32[2,65536]{0,1:T(8,128)} fusion(f32[2,65536]{0,1:T(8,128)} %bitcast.74, s32[16384]{0:T(1024)S(1)} %bitcast.80, f32[16384,2]{1,0:T(8,128)} %copy.37), kind=kCustom, calls=%fused_computation | custom fusion | flops 32768 | bytes 458752 | tf_op jit(solution)/shard_map/scatter-add | solution.py:86
  157.7 17.1 %convert_element_type.54 = bf16[2,65536]{0,1:T(8,128)(2,1)} convert(f32[2,65536]{0,1:T(8,128)} %scatter_fusion) | non-fusion elementwise | flops 131072 | bytes 786432 | tf_op jit(solution)/shard_map/convert_element_type | solution.py:87
  174.8 0.0 copy-start.3
  174.8 13.4 %copy.38 = bf16[2,64,8,128]{3,2,0,1:T(8,128)(2,1)} copy(bf16[2,64,8,128]{0,3,2,1:T(8,128)(2,1)} %bitcast.75) | data formatting | bytes 524288 | tf_op jit(solution)/shard_map/reshape | solution.py:87
  188.2 4.7 %all-to-all-start = ((bf16[2,64,8,128]{3,2,0,1:T(8,128)(2,1)}), bf16[2,64,8,128]{3,2,0,1:T(8,128)(2,1)S(1)}, u32[]{:S(2)}, u32[]{:S(2)}) async-start(bf16[2,64,8,128]{3,2,0,1:T(8,128)(2,1)} %copy.38), calls=%async_computation | async-start | bytes 524288 | tf_op jit(solution)/shard_map/all_to_all | solution.py:91
  192.8 0.1 iota_add_fusion
  192.9 0.1 convert_negate_fusion
  193.0 0.1 convert_compare_fusion
  193.2 0.0 copy-done.3
  193.2 0.6 select_convert_fusion
  193.8 5.5 %all-to-all-done = bf16[2,64,8,128]{3,2,0,1:T(8,128)(2,1)S(1)} async-done(((bf16[2,64,8,128]{3,2,0,1:T(8,128)(2,1)}), bf16[2,64,8,128]{3,2,0,1:T(8,128)(2,1)S(1)}, u32[]{:S(2)}, u32[]{:S(2)}) %all-to-all-start) | async-done | bytes 262176 | tf_op jit(solution)/shard_map/all_to_all | solution.py:91
  199.3 0.2 copy.40
  199.5 0.1 all_to_all.29
  199.7 0.1 fusion.26
  199.8 0.0 copy-start.4
  199.8 0.3 fusion.10
  200.0 0.3 convolution_add_fusion.1
  200.3 0.3 fusion.4
  200.6 4.5 %collective-permute-start = (bf16[2,4,8,2048]{3,2,1,0:T(8,128)(2,1)S(1)}, bf16[2,4,8,2048]{3,2,1,0:T(8,128)(2,1)S(1)}, u32[]{:S(2)}, u32[]{:S(2)}) collective-permute-start(bf16[2,4,8,2048]{3,2,1,0:T(8,128)(2,1)S(1)} %bitcast.81), channel_id=1, source_target_pairs={{0,16},{16,32},{32,48},{48,64},{64,80},{80,96},{96,112},{112,128},... | collective-permute-start | bytes 786440 | tf_op jit(solution)/shard_map/ppermute | solution.py:18
  205.1 3.2 %collective-permute-start.1 = (bf16[2,4,8,2048]{3,2,1,0:T(8,128)(2,1)S(1)}, bf16[2,4,8,2048]{3,2,1,0:T(8,128)(2,1)S(1)}, u32[]{:S(2)}, u32[]{:S(2)}) collective-permute-start(bf16[2,4,8,2048]{3,2,1,0:T(8,128)(2,1)S(1)} %bitcast.82), channel_id=1, source_target_pairs={{16,0},{32,16},{48,32},{64,48},{80,64},{96,80},{112,96},{128,112},... | collective-permute-start | bytes 786440 | tf_op jit(solution)/shard_map/ppermute | solution.py:20
  208.4 10.3 %collective-permute-done = bf16[2,4,8,2048]{3,2,1,0:T(8,128)(2,1)S(1)} collective-permute-done((bf16[2,4,8,2048]{3,2,1,0:T(8,128)(2,1)S(1)}, bf16[2,4,8,2048]{3,2,1,0:T(8,128)(2,1)S(1)}, u32[]{:S(2)}, u32[]{:S(2)}) %collective-permute-start) | collective-permute-done | bytes 262176 | tf_op jit(solution)/shard_map/ppermute | solution.py:18
  218.7 0.0 collective-permute-done.1
  218.7 0.0 copy-done.4
  218.7 0.3 fusion
  219.0 4.7 %copy.45 = bf16[2,4,8,2048]{2,1,0,3:T(4,128)(2,1)} copy(bf16[2,4,8,2048]{3,2,1,0:T(8,128)(2,1)S(1)} %fusion) | data formatting | bytes 524288 | tf_op jit(solution)/shard_map/convert_element_type | solution.py:68
  223.7 5.8 %reshape.135 = bf16[16,2,4096]{2,1,0:T(2,128)(2,1)S(1)} reshape(bf16[2048,2,4,8]{3,2,1,0:T(4,128)(2,1)} %bitcast.76) | data formatting | bytes 524288
  229.5 10.4 %all_to_all.36 = bf16[16,2,4096]{2,1,0:T(2,128)(2,1)S(1)} all-to-all(bf16[16,2,4096]{2,1,0:T(2,128)(2,1)S(1)} %reshape.135), channel_id=1, replica_groups=mesh['ry'=32,'rx'=16] {'rx'}, dimensions={0} | all-to-all | bytes 524288 | tf_op jit(solution)/shard_map/all_to_all | solution.py:100
  239.9 5.9 %reshape.136 = bf16[2048,2,4,8]{3,2,1,0:T(4,128)(2,1)} reshape(bf16[16,2,4096]{2,1,0:T(2,128)(2,1)S(1)} %all_to_all.36) | data formatting | bytes 524288
  245.8 0.0 copy-start.2
  245.8 6.0 %copy.46 = bf16[2,4,8,16,128]{4,1,3,2,0:T(4,128)(2,1)S(1)} copy(bf16[2,4,8,16,128]{2,1,0,4,3:T(4,128)(2,1)} %bitcast.77) | data formatting | bytes 524288 | tf_op jit(solution)/shard_map/all_to_all | solution.py:100
  251.8 0.0 copy-done
  251.8 0.0 copy-done.2
  251.8 0.2 fusion.3
  252.0 0.9 copy.47
  (4 shorter events, 0.1 us)
Async XLA Ops:
  0.0 251.8 %copy-start = (bf16[2,64,64]{2,1,0:T(8,128)(2,1)S(1)}, bf16[2,64,64]{2,1,0:T(8,128)(2,1)}, u32[]{:S(2)}) copy-start(bf16[2,64,64]{2,1,0:T(8,128)(2,1)} %param.17) | copy-start | bytes 49156
  38.5 4.9 %copy-start.1 = (bf16[2,64,8,128]{3,2,1,0:T(8,128)(2,1)S(1)}, bf16[2,64,8,128]{3,2,1,0:T(8,128)(2,1)}, u32[]{:S(2)}) copy-start(bf16[2,64,8,128]{3,2,1,0:T(8,128)(2,1)} %param.10) | copy-start | bytes 786436
  174.8 18.4 %copy-start.3 = (f32[2048]{0:T(1024)S(1)}, f32[2048]{0:T(1024)}, u32[]{:S(2)}) copy-start(f32[2048]{0:T(1024)} %param.15) | copy-start | bytes 24580
  188.2 11.1 %all-to-all-start = ((bf16[2,64,8,128]{3,2,0,1:T(8,128)(2,1)}), bf16[2,64,8,128]{3,2,0,1:T(8,128)(2,1)S(1)}, u32[]{:S(2)}, u32[]{:S(2)}) async-start(bf16[2,64,8,128]{3,2,0,1:T(8,128)(2,1)} %copy.38), calls=%async_computation | async-start | bytes 524288 | tf_op jit(solution)/shard_map/all_to_all | solution.py:91
  199.8 18.9 %copy-start.4 = (f32[8]{0:T(128)S(1)}, f32[8]{0:T(128)}, u32[]{:S(2)}) copy-start(f32[8]{0:T(128)} %param.16) | copy-start | bytes 100
  200.6 18.0 %collective-permute-start = (bf16[2,4,8,2048]{3,2,1,0:T(8,128)(2,1)S(1)}, bf16[2,4,8,2048]{3,2,1,0:T(8,128)(2,1)S(1)}, u32[]{:S(2)}, u32[]{:S(2)}) collective-permute-start(bf16[2,4,8,2048]{3,2,1,0:T(8,128)(2,1)S(1)} %bitcast.81), channel_id=1, source_target_pairs={{0,16},{16,32},{32,48},{48,64},{64,80},{80,96},{96,112},{112,128},... | collective-permute-start | bytes 786440 | tf_op jit(solution)/shard_map/ppermute | solution.py:18
  205.1 13.5 %collective-permute-start.1 = (bf16[2,4,8,2048]{3,2,1,0:T(8,128)(2,1)S(1)}, bf16[2,4,8,2048]{3,2,1,0:T(8,128)(2,1)S(1)}, u32[]{:S(2)}, u32[]{:S(2)}) collective-permute-start(bf16[2,4,8,2048]{3,2,1,0:T(8,128)(2,1)S(1)} %bitcast.82), channel_id=1, source_target_pairs={{16,0},{32,16},{48,32},{64,48},{80,64},{96,80},{112,96},{128,112},... | collective-permute-start | bytes 786440 | tf_op jit(solution)/shard_map/ppermute | solution.py:20
  245.8 6.0 %copy-start.2 = (bf16[2,64,8,128]{3,2,1,0:T(8,128)(2,1)S(1)}, bf16[2,64,8,128]{3,2,1,0:T(8,128)(2,1)}, u32[]{:S(2)}) copy-start(bf16[2,64,8,128]{3,2,1,0:T(8,128)(2,1)} %param.9) | copy-start | bytes 786436
where the time goes:
time: 256 us; the launch traced here: 253 us
  other arithmetic  120 us (47%)
  local copies, waits for them, and re-layouts  55.9 us (22%)
  blocking collectives  46.5 us (18%)
  waiting for transfers between devices  15.8 us (6%)
  starting transfers between devices  12.4 us (5%)
    scatter-add x1, other arithmetic, body(): scatter_field = base.at[:, cell_ids].add(values)  100 us
    all_gather x1, blocking collectives, body(): lax.all_gather(places, 'rx', axis=1, tiled=True)  19.2 us
    convert_element_type x1, other arithmetic, body(): scatter_field.astype(jnp.bfloat16)  17.1 us
    all_gather x1, blocking collectives, body(): lax.all_gather(obs_value, 'rx', axis=1, tiled=True)  16.9 us
    reshape x1, local copies, waits for them, and re-layouts, body(): forcing.astype(jnp.float32)  13.9 us
    reshape x1, local copies, waits for them, and re-layouts, body(): scatter_field.astype(jnp.bfloat16)  13.4 us
    unnamed x12, local copies, waits for them, and re-layouts  11.7 us
    all_to_all x1, blocking collectives, body(): lax.all_to_all(lat_smooth, 'rx', split_axis=3, concat_axis=1, tiled=True)  10.4 us
  transfers between devices with their start and end apart: 3, of which 2 were waited for; matrix products, arithmetic and copies ran while one was open for 0% of the time, Pallas kernels for 0%

commit v1 on v0

v1 whole, which is shorter than its diff:
```python
import functools

import jax
import jax.numpy as jnp
from jax import lax
from jax.experimental import pallas as pl
from jax.experimental.pallas import tpu as pltpu
from jax.sharding import PartitionSpec as P

LEV = 64
CY = 8
CX = 128
SLOTS = 1024
ROWS = LEV * CY
TILES = 16
CHUNK = 256
VMEM = pl.BlockSpec(memory_space=pltpu.VMEM)
SMEM = pl.BlockSpec(memory_space=pltpu.SMEM)
F32 = jnp.float32
BF16 = jnp.bfloat16


def iota(shape, axis):
    return lax.broadcasted_iota(jnp.int32, shape, axis)


def pack_kernel(count_ref, tile_ref, cell_ref, value_ref, out_ref):
    used = iota((1, SLOTS), 1) < count_ref[0]
    cell = cell_ref[...]
    place = (cell // CX).astype(F32)
    column = (tile_ref[...] * CX + cell % CX).astype(F32)
    values = jnp.where(used, value_ref[...], 0.0)
    block = jnp.concatenate([place, column, values], axis=0)
    for tile in range(TILES):
        out_ref[tile] = block


def factors_kernel(where_ref, rate_y_ref, rate_x_ref, vert_ref, x_ref, rate_ref, y_ref):
    band, bands = where_ref[0], where_ref[1]
    tile, tiles = where_ref[2], where_ref[3]
    rates = rate_x_ref[...]
    source = iota((CX, CX), 0)
    target = iota((CX, CX), 1)
    for part in range(3):
        far = jnp.abs(source + (part - 1) * CX - target)
        near = far <= CX
        if part == 0:
            near = jnp.logical_and(near, tile > 0)
        if part == 2:
            near = jnp.logical_and(near, tile < tiles - 1)
        weight = jnp.where(near, jnp.exp(-far.astype(F32) * rates / CX), 0.0)
        x_ref[part * CX : (part + 1) * CX, :] = weight.astype(BF16)
    rate_ref[...] = jnp.broadcast_to(-rates / CX, (CX, CX)).T

    row = iota((CY, CX), 0)
    other = iota((CY, CX), 1) % CY
    rate = jnp.zeros((CY, CX), F32)
    for y in range(CY):
        rate = jnp.where(row == y, rate_y_ref[y], rate)
    spread = (iota((ROWS, LEV), 0) // CY == iota((ROWS, LEV), 1)).astype(BF16)
    weights = []
    for part in range(3):
        far = jnp.abs(other + (part - 1) * CY - row)
        near = far <= CY
        if part == 0:
            near = jnp.logical_and(near, band > 0)
        if part == 2:
            near = jnp.logical_and(near, band < bands - 1)
        weight = jnp.where(near, jnp.exp(-far.astype(F32) * rate / CY), 0.0)
        weights.append(weight.astype(BF16).astype(F32))
    for c in range(2):
        tall = jnp.dot(spread, vert_ref[c], preferred_element_type=F32).astype(BF16)
        wide = lax.dot_general(tall, spread, (((1,), (1,)), ((), ())), preferred_element_type=F32)
        wide = wide.reshape(LEV, CY, ROWS)
        for part in range(3):
            weight = jnp.concatenate([weights[part]] * (ROWS // CX), axis=1)
            product = (wide * weight[None]).reshape(ROWS, ROWS)
            y_ref[c, :, part * ROWS : (part + 1) * ROWS] = product.astype(BF16)


def lon_kernel(where_ref, record_ref, own_ref, left_ref, right_ref, x_ref, rate_ref, out_ref, sum_ref):
    start = (where_ref[2] * CX).astype(F32)
    places = iota((ROWS, CHUNK), 0).astype(F32)
    columns = iota((CX, CHUNK), 0).astype(F32) + start
    rate = rate_ref[:, 0:1]
    sum_ref[...] = jnp.zeros_like(sum_ref)

    def step(source, carry):
        for chunk in range(SLOTS // CHUNK):
            at = slice(chunk * CHUNK, (chunk + 1) * CHUNK)
            record = record_ref[source, :, at]
            hit = jnp.where(places == record[0:1], 1.0, 0.0).astype(BF16)
            far = jnp.abs(columns - record[1:2])
            weight = jnp.where(far <= CX, jnp.exp(far * rate), 0.0)
            spread = jnp.concatenate([weight * record[2:3], weight * record[3:4]], axis=0)
            sum_ref[...] += lax.dot_general(
                hit, spread.astype(BF16), (((1,), (1,)), ((), ())), preferred_element_type=F32
            )
        return carry

    lax.fori_loop(0, TILES, step, 0)
    for c in range(2):
        at = slice(c * ROWS, (c + 1) * ROWS)
        dense = jnp.dot(left_ref[at], x_ref[0:CX], preferred_element_type=F32)
        dense += jnp.dot(own_ref[at], x_ref[CX : 2 * CX], preferred_element_type=F32)
        dense += jnp.dot(right_ref[at], x_ref[2 * CX :], preferred_element_type=F32)
        out_ref[at] = (dense + sum_ref[:, c * CX : (c + 1) * CX]).astype(BF16)


def final_kernel(control_ref, lower_ref, own_ref, upper_ref, y_ref, out_ref):
    for c in range(2):
        at = slice(c * ROWS, (c + 1) * ROWS)
        total = control_ref[at].astype(F32)
        for part, field in enumerate((lower_ref, own_ref, upper_ref)):
            total += jnp.dot(
                y_ref[c, :, part * ROWS : (part + 1) * ROWS], field[at], preferred_element_type=F32
            )
        out_ref[at] = total.astype(BF16)


def ring(axis, step):
    count = lax.axis_size(axis)
    return [(i, (i + step) % count) for i in range(count)]


def call(kernel, out_shape, specs, scratch=(), flops=0, moved=0):
    many = isinstance(out_shape, (list, tuple))
    return pl.pallas_call(
        kernel,
        out_shape=out_shape,
        in_specs=specs,
        out_specs=[VMEM] * len(out_shape) if many else VMEM,
        scratch_shapes=list(scratch),
        cost_estimate=pl.CostEstimate(flops=flops, bytes_accessed=moved, transcendentals=0),
        compiler_params=pltpu.CompilerParams(vmem_limit_bytes=32 * 2**20),
    )


def body(control, forcing, obs_tile, obs_cell, obs_value, obs_count, rate_x, rate_y, vert):
    shape = control.shape
    band, tile = lax.axis_index("ry"), lax.axis_index("rx")
    where = jnp.stack([band, lax.axis_size("ry"), tile, lax.axis_size("rx")]).astype(jnp.int32)
    field = jax.ShapeDtypeStruct((2 * ROWS, CX), BF16)

    packed = call(
        pack_kernel, jax.ShapeDtypeStruct((TILES, 4, SLOTS), F32), [SMEM, VMEM, VMEM, VMEM], moved=300000
    )(obs_count, obs_tile.reshape(1, SLOTS), obs_cell.reshape(1, SLOTS), obs_value)
    records = lax.all_to_all(packed, "rx", 0, 0, tiled=True)
    left = lax.ppermute(forcing, "rx", ring("rx", 1))
    right = lax.ppermute(forcing, "rx", ring("rx", -1))

    rate_here = lax.dynamic_slice_in_dim(rate_x, tile * CX, CX).reshape(1, CX)
    x_weights, rate_down, y_weights = call(
        factors_kernel,
        [
            jax.ShapeDtypeStruct((3 * CX, CX), BF16),
            jax.ShapeDtypeStruct((CX, CX), F32),
            jax.ShapeDtypeStruct((2, ROWS, 3 * ROWS), BF16),
        ],
        [SMEM, SMEM, VMEM, VMEM],
        flops=2 * 512 * 512 * 64 * 2 * 2,
        moved=4000000,
    )(where, rate_y, rate_here, vert)

    flat = (2 * ROWS, CX)
    smooth = call(
        lon_kernel,
        field,
        [SMEM] + [VMEM] * 6,
        [pltpu.VMEM((ROWS, 2 * CX), F32)],
        flops=2 * ROWS * 256 * TILES * SLOTS,
        moved=1000000,
    )(where, records, forcing.reshape(flat), left.reshape(flat), right.reshape(flat), x_weights, rate_down)

    wide = smooth.reshape(shape)
    lower = lax.ppermute(wide, "ry", ring("ry", 1))
    upper = lax.ppermute(wide, "ry", ring("ry", -1))
    out = call(final_kernel, field, [VMEM] * 5, flops=2 * 2 * ROWS * 3 * ROWS * CX, moved=4000000)(
        control.reshape(flat), lower.reshape(flat), smooth, upper.reshape(flat), y_weights
    )
    return out.reshape(shape)


def solution(mesh):
    placed = (
        P(None, None, "ry", "rx"),
        P(None, None, "ry", "rx"),
        P(("ry", "rx"), None),
        P(("ry", "rx")),
        P(None, ("ry", "rx")),
        P(("ry", "rx")),
        P(),
        P("ry"),
        P(),
    )
    return jax.shard_map(
        body, mesh=mesh, in_specs=placed, out_specs=P(None, None, "ry", "rx"), check_vma=False
    )
```

time: 256 us -> 65.4 us (0.26)
  the two profiles are of different devices: /device:TPU:24 before, /device:TPU:1 now
where the time goes in v1:
time: 65.4 us; the launch traced here: 64.8 us
  starting transfers between devices  29.2 us (45%)
  Pallas kernels  14.9 us (23%)
  waiting for transfers between devices  13.9 us (21%)
  local copies, waits for them, and re-layouts  5.97 us (9%)
  between operations  0.73 us (1%)
    ppermute x1, starting transfers between devices, body(): upper = lax.ppermute(wide, 'ry', ring('ry', -1))  11.3 us
    pallas_call x1, Pallas kernels, body(): call(lon_kernel, field, [SMEM] + [VMEM] * 6, [pltpu.VMEM((ROWS, 2 * CX),...  11.1 us
    ppermute x1, starting transfers between devices, body(): right = lax.ppermute(forcing, 'rx', ring('rx', -1))  8.91 us
    ppermute x1, waiting for transfers between devices, body(): lower = lax.ppermute(wide, 'ry', ring('ry', 1))  7.38 us
    unnamed x20, local copies, waits for them, and re-layouts  5.89 us
    all_to_all x1, starting transfers between devices, body(): records = lax.all_to_all(packed, 'rx', 0, 0, tiled=True)  5.14 us
    all_to_all x1, waiting for transfers between devices, body(): records = lax.all_to_all(packed, 'rx', 0, 0, tiled=True)  3.65 us
    ppermute x1, waiting for transfers between devices, body(): upper = lax.ppermute(wide, 'ry', ring('ry', -1))  2.91 us
  transfers between devices with their start and end apart: 5, of which 3 were waited for; matrix products, arithmetic and copies ran while one was open for 0% of the time, Pallas kernels for 3%

profile of v1, /device:TPU:1, one launch (start us, length us, event | category | flops | bytes accessed | tf_op | source)
XLA Modules:
  0.0 64.8 jit_solution(13342389479362800551)
XLA Ops:
  0.0 0.0 copy-start
  0.0 8.9 %collective-permute-start.1 = (bf16[2,64,8,128]{3,2,1,0:T(8,128)(2,1)}, bf16[2,64,8,128]{3,2,1,0:T(8,128)(2,1)}, u32[]{:S(2)}, u32[]{:S(2)}) collective-permute-start(bf16[2,64,8,128]{3,2,1,0:T(8,128)(2,1)} %param.10), channel_id=1, source_target_pairs={{0,15},{1,0},{2,1},{3,2},{4,3},{5,4},{6,5},{7,6},{8,7},{9,8},{10,9... | collective-permute-start | bytes 786440 | tf_op jit(solution)/shard_map/ppermute | solution.py:150
  8.9 1.9 %collective-permute-start = (bf16[2,64,8,128]{3,2,1,0:T(8,128)(2,1)}, bf16[2,64,8,128]{3,2,1,0:T(8,128)(2,1)}, u32[]{:S(2)}, u32[]{:S(2)}) collective-permute-start(bf16[2,64,8,128]{3,2,1,0:T(8,128)(2,1)} %param.10), channel_id=1, source_target_pairs={{0,1},{1,2},{2,3},{3,4},{4,5},{5,6},{6,7},{7,8},{8,9},{9,10},{10,1... | collective-permute-start | bytes 786440 | tf_op jit(solution)/shard_map/ppermute | solution.py:149
  11.5 0.0 copy-start.2
  11.5 0.7 %copy-done.2 = f32[2,1024]{1,0:T(2,128)S(1)} copy-done((f32[2,1024]{1,0:T(2,128)S(1)}, f32[2,1024]{1,0:T(2,128)}, u32[]{:S(2)}) %copy-start.2) | copy-done | bytes 8216
  12.2 0.0 copy-start.3
  12.2 0.7 %copy-done.3 = s32[1024,1]{0,1:T(1,128)S(1)} copy-done((s32[1024,1]{0,1:T(1,128)S(1)}, s32[1024,1]{0,1:T(1,128)}, u32[]{:S(2)}) %copy-start.3) | copy-done | bytes 4120
  12.9 0.0 copy-start.4
  12.9 0.7 %copy-done.4 = s32[1024]{0:T(1024)S(1)} copy-done((s32[1024]{0:T(1024)S(1)}, s32[1024]{0:T(1024)}, u32[]{:S(2)}) %copy-start.4) | copy-done | bytes 4120
  13.6 0.7 %shard_map.91 = f32[16,4,1024]{2,1,0:T(4,128)} custom-call(s32[1]{0:T(128)S(6)} %copy.10.count_ref, s32[1,1024]{1,0:T(1,128)S(1)} %bitcast.19, s32[1,1024]{1,0:T(1,128)S(1)} %bitcast.20, f32[2,1024]{1,0:T(2,128)S(1)} %copy-done.2), custom_call_target="tpu_custom_call" | custom-call | bytes 300000 | tf_op jit(solution)/shard_map/pallas_call | solution.py:145
  14.3 5.1 %all-to-all-start = ((f32[16,4,1024]{2,1,0:T(4,128)}), f32[16,4,1024]{2,1,0:T(4,128)S(1)}, u32[]{:S(2)}, u32[]{:S(2)}) async-start(f32[16,4,1024]{2,1,0:T(4,128)} %shard_map.91), calls=%async_computation | async-start | bytes 524288 | tf_op jit(solution)/shard_map/all_to_all | solution.py:148
  19.5 0.0 copy-done
  19.5 0.1 dynamic-slice_bitcast_fusion.rate_x_ref
  19.5 0.1 pad_add_fusion.where_ref
  19.6 0.0 copy-start.6
  19.6 0.8 %copy-done.6 = bf16[2,64,64]{2,1,0:T(8,128)(2,1)S(1)} copy-done((bf16[2,64,64]{2,1,0:T(8,128)(2,1)S(1)}, bf16[2,64,64]{2,1,0:T(8,128)(2,1)}, u32[]{:S(2)}) %copy-start.6) | copy-done | bytes 16408
  20.4 0.0 copy-start.7
  20.4 0.7 %copy-done.7 = f32[8]{0:T(128)S(1)} copy-done((f32[8]{0:T(128)S(1)}, f32[8]{0:T(128)}, u32[]{:S(2)}) %copy-start.7) | copy-done | bytes 56
  21.0 1.3 %shard_map.92 = (bf16[384,128]{1,0:T(8,128)(2,1)S(1)}, f32[128,128]{1,0:T(8,128)S(1)}, bf16[2,512,1536]{2,1,0:T(8,128)(2,1)S(1)}) custom-call(s32[4]{0:T(128)S(1)} %pad_add_fusion.where_ref, f32[8]{0:T(128)S(1)} %copy-done.7, f32[1,128]{1,0:T(1,128)S(1)} %dynamic-slice_bitcast_fusion.rate_x_ref, bf16[2,64,64]{2,1,0:T(8,128)(2,1)S(1)} %copy-done.6), custom_call_target="tpu_custom_call" | custom-call | flops 134217728 | bytes 4000000 | tf_op jit(solution)/shard_map/pallas_call | solution.py:153
  22.3 0.0 copy-start.8
  22.4 0.6 copy-done.8
  23.0 3.7 %all-to-all-done.record_ref = f32[16,4,1024]{2,1,0:T(4,128)S(1)} async-done(((f32[16,4,1024]{2,1,0:T(4,128)}), f32[16,4,1024]{2,1,0:T(4,128)S(1)}, u32[]{:S(2)}, u32[]{:S(2)}) %all-to-all-start) | async-done | bytes 262176 | tf_op jit(solution)/shard_map/all_to_all | solution.py:148
  26.6 0.0 collective-permute-done.1
  26.6 0.0 collective-permute-done
  26.6 0.0 copy-start.5
  26.6 0.9 %copy-done.5 = bf16[2,64,8,128]{3,2,1,0:T(8,128)(2,1)S(1)} copy-done((bf16[2,64,8,128]{3,2,1,0:T(8,128)(2,1)S(1)}, bf16[2,64,8,128]{3,2,1,0:T(8,128)(2,1)}, u32[]{:S(2)}) %copy-start.5) | copy-done | bytes 262168
  27.6 0.0 copy-start.9
  27.6 0.8 %copy-done.9 = f32[128,128]{1,0:T(8,128)S(1)} copy-done((f32[128,128]{1,0:T(8,128)S(1)}, f32[128,128]{1,0:T(8,128)}, u32[]{:S(2)}) %copy-start.9) | copy-done | bytes 65560
  28.4 0.0 copy-start.1
  28.4 11.1 %shard_map.93.own_ref = bf16[1024,128]{1,0:T(8,128)(2,1)S(1)} custom-call(s32[4]{0:T(128)S(1)} %pad_add_fusion.where_ref, f32[16,4,1024]{2,1,0:T(4,128)S(1)} %all-to-all-done.record_ref, bf16[1024,128]{1,0:T(8,128)(2,1)S(1)} %bitcast.21, bf16[1024,128]{1,0:T(8,128)(2,1)} %bitcast.6.left_ref, bf16[1024,128]{1,0:T(8,128)(2,1)} %bitcast.7.right_ref, ...), custom_call_target="tpu_custom_call" | custom-call | flops 4294967296 | bytes 1000000 | tf_op jit(solution)/shard_map/pallas_call | solution.py:166
  39.6 11.3 %collective-permute-start.3 = (bf16[2,64,8,128]{3,2,1,0:T(8,128)(2,1)S(1)}, bf16[2,64,8,128]{3,2,1,0:T(8,128)(2,1)S(1)}, u32[]{:S(2)}, u32[]{:S(2)}) collective-permute-start(bf16[2,64,8,128]{3,2,1,0:T(8,128)(2,1)S(1)} %bitcast.15), channel_id=1, source_target_pairs={{0,496},{16,0},{32,16},{48,32},{64,48},{80,64},{96,80},{112,96},{1... | collective-permute-start | bytes 786440 | tf_op jit(solution)/shard_map/ppermute | solution.py:177
  50.9 1.9 %collective-permute-start.2 = (bf16[2,64,8,128]{3,2,1,0:T(8,128)(2,1)S(1)}, bf16[2,64,8,128]{3,2,1,0:T(8,128)(2,1)S(1)}, u32[]{:S(2)}, u32[]{:S(2)}) collective-permute-start(bf16[2,64,8,128]{3,2,1,0:T(8,128)(2,1)S(1)} %bitcast.16), channel_id=1, source_target_pairs={{0,16},{16,32},{32,48},{48,64},{64,80},{80,96},{96,112},{112,128},... | collective-permute-start | bytes 786440 | tf_op jit(solution)/shard_map/ppermute | solution.py:176
  52.8 2.9 %collective-permute-done.3 = bf16[2,64,8,128]{3,2,1,0:T(8,128)(2,1)S(1)} collective-permute-done((bf16[2,64,8,128]{3,2,1,0:T(8,128)(2,1)S(1)}, bf16[2,64,8,128]{3,2,1,0:T(8,128)(2,1)S(1)}, u32[]{:S(2)}, u32[]{:S(2)}) %collective-permute-start.3) | collective-permute-done | bytes 262176 | tf_op jit(solution)/shard_map/ppermute | solution.py:177
  55.7 7.4 %collective-permute-done.2 = bf16[2,64,8,128]{3,2,1,0:T(8,128)(2,1)S(1)} collective-permute-done((bf16[2,64,8,128]{3,2,1,0:T(8,128)(2,1)S(1)}, bf16[2,64,8,128]{3,2,1,0:T(8,128)(2,1)S(1)}, u32[]{:S(2)}, u32[]{:S(2)}) %collective-permute-start.2) | collective-permute-done | bytes 262176 | tf_op jit(solution)/shard_map/ppermute | solution.py:176
  63.1 0.0 copy-done.1
  63.1 1.7 %shard_map.94 = bf16[1024,128]{1,0:T(8,128)(2,1)} custom-call(bf16[1024,128]{1,0:T(8,128)(2,1)S(1)} %bitcast.14, bf16[1024,128]{1,0:T(8,128)(2,1)S(1)} %bitcast.18, bf16[1024,128]{1,0:T(8,128)(2,1)S(1)} %shard_map.93.own_ref, bf16[1024,128]{1,0:T(8,128)(2,1)S(1)} %bitcast.17, bf16[2,512,1536]{2,1,0:T(8,128)(2,1)S(1)} %get-tuple-element.10.y_ref), custom_call_target="tpu_custom_call" | custom-call | flops 402653184 | bytes 4000000 | tf_op jit(solution)/shard_map/pallas_call | solution.py:178
Async XLA Ops:
  0.0 19.5 %copy-start = (f32[2048]{0:T(1024)S(1)}, f32[2048]{0:T(1024)}, u32[]{:S(2)}) copy-start(f32[2048]{0:T(1024)} %param.15) | copy-start | bytes 24580
  0.0 26.6 %collective-permute-start.1 = (bf16[2,64,8,128]{3,2,1,0:T(8,128)(2,1)}, bf16[2,64,8,128]{3,2,1,0:T(8,128)(2,1)}, u32[]{:S(2)}, u32[]{:S(2)}) collective-permute-start(bf16[2,64,8,128]{3,2,1,0:T(8,128)(2,1)} %param.10), channel_id=1, source_target_pairs={{0,15},{1,0},{2,1},{3,2},{4,3},{5,4},{6,5},{7,6},{8,7},{9,8},{10,9... | collective-permute-start | bytes 786440 | tf_op jit(solution)/shard_map/ppermute | solution.py:150
  8.9 17.7 %collective-permute-start = (bf16[2,64,8,128]{3,2,1,0:T(8,128)(2,1)}, bf16[2,64,8,128]{3,2,1,0:T(8,128)(2,1)}, u32[]{:S(2)}, u32[]{:S(2)}) collective-permute-start(bf16[2,64,8,128]{3,2,1,0:T(8,128)(2,1)} %param.10), channel_id=1, source_target_pairs={{0,1},{1,2},{2,3},{3,4},{4,5},{5,6},{6,7},{7,8},{8,9},{9,10},{10,1... | collective-permute-start | bytes 786440 | tf_op jit(solution)/shard_map/ppermute | solution.py:149
  11.5 0.7 %copy-start.2 = (f32[2,1024]{1,0:T(2,128)S(1)}, f32[2,1024]{1,0:T(2,128)}, u32[]{:S(2)}) copy-start(f32[2,1024]{1,0:T(2,128)} %value_ref.1) | copy-start | bytes 24580
  12.2 0.7 %copy-start.3 = (s32[1024,1]{0,1:T(1,128)S(1)}, s32[1024,1]{0,1:T(1,128)}, u32[]{:S(2)}) copy-start(s32[1024,1]{0,1:T(1,128)} %param.11) | copy-start | bytes 12292
  12.9 0.7 %copy-start.4 = (s32[1024]{0:T(1024)S(1)}, s32[1024]{0:T(1024)}, u32[]{:S(2)}) copy-start(s32[1024]{0:T(1024)} %param.12) | copy-start | bytes 12292
  14.3 12.3 %all-to-all-start = ((f32[16,4,1024]{2,1,0:T(4,128)}), f32[16,4,1024]{2,1,0:T(4,128)S(1)}, u32[]{:S(2)}, u32[]{:S(2)}) async-start(f32[16,4,1024]{2,1,0:T(4,128)} %shard_map.91), calls=%async_computation | async-start | bytes 524288 | tf_op jit(solution)/shard_map/all_to_all | solution.py:148
  19.6 0.8 %copy-start.6 = (bf16[2,64,64]{2,1,0:T(8,128)(2,1)S(1)}, bf16[2,64,64]{2,1,0:T(8,128)(2,1)}, u32[]{:S(2)}) copy-start(bf16[2,64,64]{2,1,0:T(8,128)(2,1)} %vert_ref.1) | copy-start | bytes 49156
  20.4 0.7 %copy-start.7 = (f32[8]{0:T(128)S(1)}, f32[8]{0:T(128)}, u32[]{:S(2)}) copy-start(f32[8]{0:T(128)} %rate_y_ref.1) | copy-start | bytes 100
  22.3 0.6 copy-start.8
  26.6 1.0 %copy-start.5 = (bf16[2,64,8,128]{3,2,1,0:T(8,128)(2,1)S(1)}, bf16[2,64,8,128]{3,2,1,0:T(8,128)(2,1)}, u32[]{:S(2)}) copy-start(bf16[2,64,8,128]{3,2,1,0:T(8,128)(2,1)} %param.10) | copy-start | bytes 786436
  27.6 0.8 %copy-start.9 = (f32[128,128]{1,0:T(8,128)S(1)}, f32[128,128]{1,0:T(8,128)}, u32[]{:S(2)}) copy-start(f32[128,128]{1,0:T(8,128)} %copy-done.8) | copy-start | bytes 196612
  28.4 34.6 %copy-start.1 = (bf16[2,64,8,128]{3,2,1,0:T(8,128)(2,1)S(1)}, bf16[2,64,8,128]{3,2,1,0:T(8,128)(2,1)}, u32[]{:S(2)}) copy-start(bf16[2,64,8,128]{3,2,1,0:T(8,128)(2,1)} %param.9) | copy-start | bytes 786436
  39.6 16.1 %collective-permute-start.3 = (bf16[2,64,8,128]{3,2,1,0:T(8,128)(2,1)S(1)}, bf16[2,64,8,128]{3,2,1,0:T(8,128)(2,1)S(1)}, u32[]{:S(2)}, u32[]{:S(2)}) collective-permute-start(bf16[2,64,8,128]{3,2,1,0:T(8,128)(2,1)S(1)} %bitcast.15), channel_id=1, source_target_pairs={{0,496},{16,0},{32,16},{48,32},{64,48},{80,64},{96,80},{112,96},{1... | collective-permute-start | bytes 786440 | tf_op jit(solution)/shard_map/ppermute | solution.py:177
  50.9 12.2 %collective-permute-start.2 = (bf16[2,64,8,128]{3,2,1,0:T(8,128)(2,1)S(1)}, bf16[2,64,8,128]{3,2,1,0:T(8,128)(2,1)S(1)}, u32[]{:S(2)}, u32[]{:S(2)}) collective-permute-start(bf16[2,64,8,128]{3,2,1,0:T(8,128)(2,1)S(1)} %bitcast.16), channel_id=1, source_target_pairs={{0,16},{16,32},{32,48},{48,64},{64,80},{80,96},{96,112},{112,128},... | collective-permute-start | bytes 786440 | tf_op jit(solution)/shard_map/ppermute | solution.py:176

commit v2 on v1

v2 whole, which is shorter than its diff:
```python
import jax
import jax.numpy as jnp
from jax import lax
from jax.experimental import pallas as pl
from jax.experimental.pallas import tpu as pltpu
from jax.sharding import PartitionSpec as P

LEV = 64
CY = 8
CX = 128
SLOTS = 1024
ROWS = LEV * CY
TILES = 16
PARTS = SLOTS // CX
VMEM = pl.BlockSpec(memory_space=pltpu.VMEM)
HBM = pl.BlockSpec(memory_space=pltpu.HBM)
F32 = jnp.float32
BF16 = jnp.bfloat16
I32 = jnp.int32
ACROSS = (((1,), (1,)), ((), ()))


def iota(shape, axis):
    return lax.broadcasted_iota(I32, shape, axis)


def pack_kernel(count_ref, place_ref, value_ref, out_ref, field_ref, lane_ref):
    before = (iota((CX, CX), 0) <= iota((CX, CX), 1)).astype(F32).astype(BF16)
    above = (iota((CX, CX), 0) > iota((CX, CX), 1)).astype(F32).astype(BF16)
    slot = iota((PARTS, CX), 0) * CX + iota((PARTS, CX), 1)
    used = slot < count_ref[...]
    tile = jnp.where(used, place_ref[0], -1)
    cell = place_ref[1]
    fields = [
        (cell // CX - ROWS // 2).astype(F32),
        (tile + 1).astype(F32),
        (cell % CX - CX // 2).astype(F32),
        value_ref[0:1].reshape(PARTS, CX),
        value_ref[1:2].reshape(PARTS, CX),
    ]

    named = jnp.concatenate([jnp.where(tile == t, 1.0, 0.0) for t in range(TILES)], axis=0)
    within = jnp.dot(named.astype(BF16), before, preferred_element_type=F32)
    counts = jnp.broadcast_to(within[:, CX - 1 :], (CX, CX)).astype(BF16)
    rank = named * (within + jnp.dot(above, counts, preferred_element_type=F32) - 1.0)
    rank = jnp.sum(rank.reshape(TILES, PARTS, CX), axis=0)
    rank = jnp.where(used, rank, float(SLOTS)).astype(I32)

    row, lane = rank // CX, rank % CX
    for part in range(PARTS):
        at = slice(part * CX, (part + 1) * CX)
        here = iota((PARTS, CX), 0) == row[part : part + 1]
        for i, field in enumerate(fields):
            picked = jnp.where(here, field[part : part + 1], 0.0)
            field_ref[i * PARTS : (i + 1) * PARTS, at] = picked.astype(BF16)
        lane_ref[:, at] = jnp.where(iota((CX, CX), 0) == lane[part : part + 1], 1.0, 0.0).astype(BF16)
    ordered = lax.dot_general(field_ref[...], lane_ref[...], ACROSS, preferred_element_type=F32)
    place, named, column, first, second = (ordered[i * PARTS : (i + 1) * PARTS] for i in range(5))
    column = jnp.where(named > 0.0, (named - 1.0) * CX + column, 4.0 * TILES * CX)
    for t in range(TILES):
        out_ref[t] = jnp.concatenate([place, column - t * CX, first, second], axis=0).astype(BF16)


def lon_kernel(
    record_ref, own_hbm, rate_x_hbm, sum_ref, x_ref, own_ref, rate_x_ref, rate_ref, list_ref, hit_ref, spread_ref, sems
):
    copies = [
        pltpu.make_async_copy(rate_x_hbm, rate_x_ref, sems.at[0]),
        pltpu.make_async_copy(own_hbm, own_ref, sems.at[1]),
    ]
    for copy in copies:
        copy.start()

    rows = TILES * PARTS
    field = lambda f: record_ref[:, f * PARTS : (f + 1) * PARTS, :].reshape(rows, CX)
    column = field(1).astype(F32)
    reached = jnp.logical_and(column >= -1.5 * CX, column < 1.5 * CX)
    some = jnp.max(jnp.where(reached, 1.0, 0.0), axis=1, keepdims=True)
    some = jnp.broadcast_to(some, (rows, CX)).astype(BF16)
    across = (((0,), (0,)), ((), ()))
    upto = (iota((rows, rows), 0) <= iota((rows, rows), 1)).astype(F32).astype(BF16)
    under = (iota((rows, rows), 0) < iota((rows, rows), 1)).astype(F32).astype(BF16)
    upto = lax.dot_general(some, upto, across, preferred_element_type=F32)
    under = lax.dot_general(some, under, across, preferred_element_type=F32)
    target_row = iota((rows, rows), 0).astype(F32)
    moved = jnp.logical_and(under == target_row, upto == target_row + 1.0)
    moved = jnp.where(moved, 1.0, 0.0).astype(BF16)
    for f in range(4):
        list_ref[f] = jnp.dot(moved, field(f), preferred_element_type=F32)
    used_rows = jnp.max(upto).astype(I32)

    tile, tiles = lax.axis_index("rx"), lax.axis_size("rx")
    copies[0].wait()
    rates = rate_x_ref[pl.ds(tile, 1), :]
    source = iota((CX, CX), 0)
    target = iota((CX, CX), 1)
    weights = []
    for part in range(3):
        far = jnp.abs(source + (part - 1) * CX - target)
        near = far <= CX
        if part == 0:
            near = jnp.logical_and(near, tile > 0)
        if part == 2:
            near = jnp.logical_and(near, tile < tiles - 1)
        weights.append(jnp.where(near, jnp.exp(-far.astype(F32) * rates / CX), 0.0))
    even = tile % 2 == 0
    x_ref[0:CX] = jnp.where(even, weights[2], weights[0]).astype(BF16)
    x_ref[CX : 2 * CX] = jnp.where(even, weights[0], weights[2]).astype(BF16)
    middle = weights[1].astype(BF16)
    rate_ref[...] = jnp.broadcast_to(rates * (-1.0 / CX), (CX, CX)).T
    copies[1].wait()
    for c in range(2):
        sum_ref[:, c * CX : (c + 1) * CX] = jnp.dot(
            own_ref[c * ROWS : (c + 1) * ROWS], middle, preferred_element_type=F32
        )

    def step(i, carry):
        record = list_ref[:, pl.ds(pl.multiple_of(i * PARTS, PARTS), PARTS), :]
        places = iota((ROWS, CX), 0) - ROWS // 2
        columns = (iota((CX, CX), 0) - CX // 2).astype(F32)
        for part in range(PARTS):
            at = slice(part * CX, (part + 1) * CX)
            row = lambda f: record[f, part : part + 1]
            hit_ref[:, at] = jnp.where(places == row(0).astype(I32), 1.0, 0.0).astype(BF16)
            far = jnp.abs(columns - row(1))
            weight = jnp.where(far <= CX, jnp.exp(far * rate_ref[...]), 0.0)
            for c in range(2):
                spread_ref[c * CX : (c + 1) * CX, at] = (weight * row(2 + c)).astype(BF16)
        sum_ref[...] += lax.dot_general(hit_ref[...], spread_ref[...], ACROSS, preferred_element_type=F32)
        return carry

    lax.fori_loop(0, (used_rows + PARTS - 1) // PARTS, step, 0)


def dense_kernel(sum_ref, near_ref, far_ref, x_ref, out_ref):
    for c in range(2):
        at = slice(c * ROWS, (c + 1) * ROWS)
        total = sum_ref[:, c * CX : (c + 1) * CX]
        total += jnp.dot(near_ref[at], x_ref[0:CX], preferred_element_type=F32)
        total += jnp.dot(far_ref[at], x_ref[CX : 2 * CX], preferred_element_type=F32)
        out_ref[at] = total.astype(BF16)


def own_kernel(smooth_ref, control_ref, rate_y_ref, vert_ref, total_ref, y_ref):
    band, bands = lax.axis_index("ry"), lax.axis_size("ry")
    row = iota((CY, CX), 0)
    other = iota((CY, CX), 1) % CY
    rate = jnp.zeros((CY, CX), F32)
    for y in range(CY):
        rate = jnp.where(row == y, rate_y_ref[0:1, y : y + 1], rate)
    spread = (iota((ROWS, LEV), 0) // CY == iota((ROWS, LEV), 1)).astype(BF16)
    weights = []
    for part in range(3):
        far = jnp.abs(other + (part - 1) * CY - row)
        near = far <= CY
        if part == 0:
            near = jnp.logical_and(near, band > 0)
        if part == 2:
            near = jnp.logical_and(near, band < bands - 1)
        weight = jnp.where(near, jnp.exp(-far.astype(F32) * rate / CY), 0.0)
        weights.append(jnp.concatenate([weight.astype(BF16).astype(F32)] * (ROWS // CX), axis=1))
    for c in range(2):
        at = slice(c * ROWS, (c + 1) * ROWS)
        tall = jnp.dot(spread, vert_ref[c], preferred_element_type=F32).astype(BF16)
        wide = lax.dot_general(tall, spread, ACROSS, preferred_element_type=F32).reshape(LEV, CY, ROWS)
        for part in (0, 2):
            product = (wide * weights[part][None]).reshape(ROWS, ROWS)
            y_ref[c, :, part // 2 * ROWS : (part // 2 + 1) * ROWS] = product.astype(BF16)
        middle = (wide * weights[1][None]).reshape(ROWS, ROWS).astype(BF16)
        mixed = jnp.dot(middle, smooth_ref[at], preferred_element_type=F32)
        total_ref[at] = control_ref[at].astype(F32) + mixed


def final_kernel(total_ref, lower_ref, upper_ref, y_ref, out_ref):
    for c in range(2):
        at = slice(c * ROWS, (c + 1) * ROWS)
        total = total_ref[at]
        total += jnp.dot(y_ref[c, :, 0:ROWS], lower_ref[at], preferred_element_type=F32)
        total += jnp.dot(y_ref[c, :, ROWS:], upper_ref[at], preferred_element_type=F32)
        out_ref[at] = total.astype(BF16)


def call(kernel, out_shape, specs, scratch=(), flops=0, moved=0, limit=24):
    many = isinstance(out_shape, (list, tuple))
    return pl.pallas_call(
        kernel,
        out_shape=out_shape,
        in_specs=specs,
        out_specs=[VMEM] * len(out_shape) if many else VMEM,
        scratch_shapes=list(scratch),
        cost_estimate=pl.CostEstimate(flops=flops, bytes_accessed=moved, transcendentals=0),
        compiler_params=pltpu.CompilerParams(vmem_limit_bytes=limit * 2**20),
    )


def body(control, forcing, obs_tile, obs_cell, obs_value, obs_count, rate_x, rate_y, vert):
    shape = control.shape
    flat = (2 * ROWS, CX)
    bands, tiles = lax.axis_size("ry"), lax.axis_size("rx")
    struct = jax.ShapeDtypeStruct

    places = jnp.stack([obs_tile.reshape(PARTS, CX), obs_cell.reshape(PARTS, CX)])
    packed = call(
        pack_kernel,
        struct((TILES, 4 * PARTS, CX), BF16),
        [VMEM] * 3,
        [pltpu.VMEM((5 * PARTS, SLOTS), BF16), pltpu.VMEM((CX, SLOTS), BF16)],
        flops=3 * 10**9,
        moved=200000,
    )(obs_count.reshape(1, 1), places, obs_value)
    records = lax.all_to_all(packed, "rx", 0, 0, tiled=True)

    held, _ = lax.optimization_barrier((forcing, packed))
    inner = lax.ppermute(held, "rx", [(i, i ^ 1) for i in range(tiles)])
    outer = lax.ppermute(held, "rx", [(i, ((i + 1) ^ 1) - 1) for i in range(1, tiles - 1)])

    total, x_weights = call(
        lon_kernel,
        [struct((ROWS, 2 * CX), F32), struct((2 * CX, CX), BF16)],
        [VMEM, HBM, HBM],
        [
            pltpu.VMEM(flat, BF16),
            pltpu.VMEM((TILES, CX), F32),
            pltpu.VMEM((CX, CX), F32),
            pltpu.VMEM((4, TILES * PARTS, CX), F32),
            pltpu.VMEM((ROWS, SLOTS), BF16),
            pltpu.VMEM((2 * CX, SLOTS), BF16),
            pltpu.SemaphoreType.DMA((2,)),
        ],
        flops=2 * ROWS * 256 * TILES * SLOTS,
        moved=1000000,
    )(records, forcing.reshape(flat), rate_x.reshape(TILES, CX))

    smooth = call(dense_kernel, struct(flat, BF16), [VMEM] * 4, flops=2 * 1024 * 256 * 128, moved=1000000)(
        total, inner.reshape(flat), outer.reshape(flat), x_weights
    )
    wide = smooth.reshape(shape)
    lower = lax.ppermute(wide, "ry", [(i, i + 1) for i in range(bands - 1)])
    upper = lax.ppermute(wide, "ry", [(i + 1, i) for i in range(bands - 1)])
    total, y_weights = call(
        own_kernel,
        [struct(flat, F32), struct((2, ROWS, 2 * ROWS), BF16)],
        [VMEM] * 4,
        flops=2 * 2 * ROWS * ROWS * CX * 2,
        moved=4000000,
    )(smooth, control.reshape(flat), rate_y.reshape(1, CY), vert)
    out = call(final_kernel, struct(flat, BF16), [VMEM] * 4, flops=2 * 2 * ROWS * 2 * ROWS * CX, moved=4000000)(
        total, lower.reshape(flat), upper.reshape(flat), y_weights
    )
    return out.reshape(shape)


def solution(mesh):
    placed = (
        P(None, None, "ry", "rx"),
        P(None, None, "ry", "rx"),
        P(("ry", "rx"), None),
        P(("ry", "rx")),
        P(None, ("ry", "rx")),
        P(("ry", "rx")),
        P(),
        P("ry"),
        P(),
    )
    return jax.shard_map(
        body, mesh=mesh, in_specs=placed, out_specs=P(None, None, "ry", "rx"), check_vma=False
    )
```

time: 65.4 us -> 41.7 us (0.64)
  the two profiles are of different devices: /device:TPU:1 before, /device:TPU:121 now
where the time goes in v2:
time: 41.7 us; the launch traced here: 41.3 us
  starting transfers between devices  21.6 us (52%)
  waiting for transfers between devices  9.47 us (23%)
  Pallas kernels  7.98 us (19%)
  between operations  0.79 us (2%)
  local copies, waits for them, and re-layouts  0.72 us (2%)
  other arithmetic  0.71 us (2%)
    all_to_all x1, starting transfers between devices, body(): records = lax.all_to_all(packed, 'rx', 0, 0, tiled=True)  6.09 us
    ppermute x1, starting transfers between devices, body(): lower = lax.ppermute(wide, 'ry', [(i, i + 1) for i in range(bands - 1)])  5.27 us
    ppermute x1, waiting for transfers between devices, body(): upper = lax.ppermute(wide, 'ry', [(i + 1, i) for i in range(bands - 1)])  5.08 us
    ppermute x1, waiting for transfers between devices, body(): lower = lax.ppermute(wide, 'ry', [(i, i + 1) for i in range(bands - 1)])  4.38 us
    pallas_call x1, Pallas kernels, body(): call(lon_kernel, [struct((ROWS, 2 * CX), F32), struct((2 * CX, CX), BF16)...  3.92 us
    ppermute x1, starting transfers between devices, body(): upper = lax.ppermute(wide, 'ry', [(i + 1, i) for i in range(bands - 1)])  3.63 us
    ppermute x1, starting transfers between devices, body(): lax.ppermute(held, 'rx', [(i, (i + 1 ^ 1) - 1) for i in range(1, tiles -...  3.34 us
    ppermute x1, starting transfers between devices, body(): inner = lax.ppermute(held, 'rx', [(i, i ^ 1) for i in range(tiles)])  3.26 us
  transfers between devices with their start and end apart: 5, of which 2 were waited for; matrix products, arithmetic and copies ran while one was open for 0% of the time, Pallas kernels for 12%

profile of v2, /device:TPU:121, one launch (start us, length us, event | category | flops | bytes accessed | tf_op | source)
XLA Modules:
  0.0 41.3 jit_solution(17840686581851098025)
XLA Ops:
  0.7 0.7 %pad_add_fusion.place_ref = s32[2,8,128]{2,1,0:T(8,128)S(1)} fusion(s32[1,8,128]{2,1,0:T(8,128)} %bitcast.24, s32[1,8,128]{2,1,0:T(8,128)} %bitcast.25), kind=kLoop, calls=%fused_computation | loop fusion | flops 2048 | bytes 16384 | tf_op jit(solution)/shard_map/stack | solution.py:202
  1.4 0.0 copy-start.3
  1.4 0.7 %copy-done.3 = f32[2,1024]{1,0:T(2,128)S(1)} copy-done((f32[2,1024]{1,0:T(2,128)S(1)}, f32[2,1024]{1,0:T(2,128)}, u32[]{:S(2)}) %copy-start.3) | copy-done | bytes 8216
  2.1 0.0 copy-start
  2.1 0.0 copy-start.4
  2.1 1.3 %shard_map.91 = bf16[16,32,128]{2,1,0:T(8,128)(2,1)} custom-call(s32[1,1]{1,0:T(1,128)} %bitcast.13.count_ref, s32[2,8,128]{2,1,0:T(8,128)S(1)} %pad_add_fusion.place_ref, f32[2,1024]{1,0:T(2,128)S(1)} %copy-done.3), custom_call_target="tpu_custom_call" | custom-call | flops 3000000000 | bytes 200000 | tf_op jit(solution)/shard_map/pallas_call | solution.py:203
  3.4 6.1 %all-to-all-start = ((bf16[16,32,128]{2,1,0:T(8,128)(2,1)}), bf16[16,32,128]{2,1,0:T(8,128)(2,1)S(1)}, u32[]{:S(2)}, u32[]{:S(2)}) async-start(bf16[16,32,128]{2,1,0:T(8,128)(2,1)} %shard_map.91), calls=%async_computation | async-start | bytes 262144 | tf_op jit(solution)/shard_map/all_to_all | solution.py:211
  9.5 0.0 copy-done
  9.5 3.3 %collective-permute-start.1 = (bf16[2,64,8,128]{3,2,1,0:T(8,128)(2,1)S(1)}, bf16[2,64,8,128]{3,2,1,0:T(8,128)(2,1)S(1)}, u32[]{:S(2)}, u32[]{:S(2)}) collective-permute-start(bf16[2,64,8,128]{3,2,1,0:T(8,128)(2,1)S(1)} %copy-done), channel_id=1, source_target_pairs={{1,2},{2,1},{3,4},{4,3},{5,6},{6,5},{7,8},{8,7},{9,10},{10,9},{11,... | collective-permute-start | bytes 786440 | tf_op jit(solution)/shard_map/ppermute | solution.py:215
  12.8 3.3 %collective-permute-start = (bf16[2,64,8,128]{3,2,1,0:T(8,128)(2,1)S(1)}, bf16[2,64,8,128]{3,2,1,0:T(8,128)(2,1)S(1)}, u32[]{:S(2)}, u32[]{:S(2)}) collective-permute-start(bf16[2,64,8,128]{3,2,1,0:T(8,128)(2,1)S(1)} %copy-done), channel_id=1, source_target_pairs={{0,1},{1,0},{2,3},{3,2},{4,5},{5,4},{6,7},{7,6},{8,9},{9,8},{10,11... | collective-permute-start | bytes 786440 | tf_op jit(solution)/shard_map/ppermute | solution.py:214
  16.1 0.0 all-to-all-done.record_ref
  16.1 0.0 copy-done.4
  16.1 0.0 copy-start.1
  16.1 0.0 copy-start.2
  16.2 0.0 copy-start.5
  16.2 3.9 %shard_map.92 = (f32[512,256]{1,0:T(8,128)S(1)}, bf16[256,128]{1,0:T(8,128)(2,1)S(1)}) custom-call(bf16[16,32,128]{2,1,0:T(8,128)(2,1)S(1)} %all-to-all-done.record_ref, bf16[1024,128]{1,0:T(8,128)(2,1)S(1)} %bitcast.20, f32[16,128]{1,0:T(8,128)S(1)} %bitcast.22), custom_call_target="tpu_custom_call" | custom-call | flops 4294967296 | bytes 1000000 | tf_op jit(solution)/shard_map/pallas_call | solution.py:217
  20.1 0.0 collective-permute-done.1
  20.1 0.0 collective-permute-done
  20.1 0.3 shard_map.93.smooth_ref
  20.4 3.6 %collective-permute-start.3 = (bf16[2,64,8,128]{3,2,1,0:T(8,128)(2,1)S(1)}, bf16[2,64,8,128]{3,2,1,0:T(8,128)(2,1)S(1)}, u32[]{:S(2)}, u32[]{:S(2)}) collective-permute-start(bf16[2,64,8,128]{3,2,1,0:T(8,128)(2,1)S(1)} %bitcast.16), channel_id=1, source_target_pairs={{16,0},{32,16},{48,32},{64,48},{80,64},{96,80},{112,96},{128,112},... | collective-permute-start | bytes 786440 | tf_op jit(solution)/shard_map/ppermute | solution.py:239
  24.0 5.3 %collective-permute-start.2 = (bf16[2,64,8,128]{3,2,1,0:T(8,128)(2,1)S(1)}, bf16[2,64,8,128]{3,2,1,0:T(8,128)(2,1)S(1)}, u32[]{:S(2)}, u32[]{:S(2)}) collective-permute-start(bf16[2,64,8,128]{3,2,1,0:T(8,128)(2,1)S(1)} %bitcast.17), channel_id=1, source_target_pairs={{0,16},{16,32},{32,48},{48,64},{64,80},{80,96},{96,112},{112,128},... | collective-permute-start | bytes 786440 | tf_op jit(solution)/shard_map/ppermute | solution.py:238
  29.3 0.0 copy-done.1
  29.3 0.0 copy-done.2
  29.3 0.0 copy-done.5
  29.3 1.0 %shard_map.94 = (f32[1024,128]{1,0:T(8,128)S(1)}, bf16[2,512,1024]{2,1,0:T(8,128)(2,1)S(1)}) custom-call(bf16[1024,128]{1,0:T(8,128)(2,1)S(1)} %shard_map.93.smooth_ref, bf16[1024,128]{1,0:T(8,128)(2,1)S(1)} %bitcast.21, f32[1,8]{1,0:T(1,128)S(1)} %bitcast.23, bf16[2,64,64]{2,1,0:T(8,128)(2,1)S(1)} %copy-done.2), custom_call_target="tpu_custom_call" | custom-call | flops 268435456 | bytes 4000000 | tf_op jit(solution)/shard_map/pallas_call | solution.py:240
  30.4 5.1 %collective-permute-done.3 = bf16[2,64,8,128]{3,2,1,0:T(8,128)(2,1)S(1)} collective-permute-done((bf16[2,64,8,128]{3,2,1,0:T(8,128)(2,1)S(1)}, bf16[2,64,8,128]{3,2,1,0:T(8,128)(2,1)S(1)}, u32[]{:S(2)}, u32[]{:S(2)}) %collective-permute-start.3) | collective-permute-done | bytes 262176 | tf_op jit(solution)/shard_map/ppermute | solution.py:239
  35.5 4.4 %collective-permute-done.2 = bf16[2,64,8,128]{3,2,1,0:T(8,128)(2,1)S(1)} collective-permute-done((bf16[2,64,8,128]{3,2,1,0:T(8,128)(2,1)S(1)}, bf16[2,64,8,128]{3,2,1,0:T(8,128)(2,1)S(1)}, u32[]{:S(2)}, u32[]{:S(2)}) %collective-permute-start.2) | collective-permute-done | bytes 262176 | tf_op jit(solution)/shard_map/ppermute | solution.py:238
  39.8 1.4 %shard_map.95 = bf16[1024,128]{1,0:T(8,128)(2,1)} custom-call(f32[1024,128]{1,0:T(8,128)S(1)} %get-tuple-element.13.total_ref, bf16[1024,128]{1,0:T(8,128)(2,1)S(1)} %bitcast.19, bf16[1024,128]{1,0:T(8,128)(2,1)S(1)} %bitcast.18, bf16[2,512,1024]{2,1,0:T(8,128)(2,1)S(1)} %get-tuple-element.14.y_ref), custom_call_target="tpu_custom_call" | custom-call | flops 268435456 | bytes 4000000 | tf_op jit(solution)/shard_map/pallas_call | solution.py:247
Async XLA Ops:
  1.4 0.7 %copy-start.3 = (f32[2,1024]{1,0:T(2,128)S(1)}, f32[2,1024]{1,0:T(2,128)}, u32[]{:S(2)}) copy-start(f32[2,1024]{1,0:T(2,128)} %value_ref.1) | copy-start | bytes 24580
  2.1 7.4 %copy-start = (bf16[2,64,8,128]{3,2,1,0:T(8,128)(2,1)S(1)}, bf16[2,64,8,128]{3,2,1,0:T(8,128)(2,1)}, u32[]{:S(2)}) copy-start(bf16[2,64,8,128]{3,2,1,0:T(8,128)(2,1)} %param.10) | copy-start | bytes 786436
  2.1 14.1 %copy-start.4 = (f32[2048]{0:T(1024)S(1)}, f32[2048]{0:T(1024)}, u32[]{:S(2)}) copy-start(f32[2048]{0:T(1024)} %param.15) | copy-start | bytes 24580
  3.4 12.7 %all-to-all-start = ((bf16[16,32,128]{2,1,0:T(8,128)(2,1)}), bf16[16,32,128]{2,1,0:T(8,128)(2,1)S(1)}, u32[]{:S(2)}, u32[]{:S(2)}) async-start(bf16[16,32,128]{2,1,0:T(8,128)(2,1)} %shard_map.91), calls=%async_computation | async-start | bytes 262144 | tf_op jit(solution)/shard_map/all_to_all | solution.py:211
  9.5 10.6 %collective-permute-start.1 = (bf16[2,64,8,128]{3,2,1,0:T(8,128)(2,1)S(1)}, bf16[2,64,8,128]{3,2,1,0:T(8,128)(2,1)S(1)}, u32[]{:S(2)}, u32[]{:S(2)}) collective-permute-start(bf16[2,64,8,128]{3,2,1,0:T(8,128)(2,1)S(1)} %copy-done), channel_id=1, source_target_pairs={{1,2},{2,1},{3,4},{4,3},{5,6},{6,5},{7,8},{8,7},{9,10},{10,9},{11,... | collective-permute-start | bytes 786440 | tf_op jit(solution)/shard_map/ppermute | solution.py:215
  12.8 7.3 %collective-permute-start = (bf16[2,64,8,128]{3,2,1,0:T(8,128)(2,1)S(1)}, bf16[2,64,8,128]{3,2,1,0:T(8,128)(2,1)S(1)}, u32[]{:S(2)}, u32[]{:S(2)}) collective-permute-start(bf16[2,64,8,128]{3,2,1,0:T(8,128)(2,1)S(1)} %copy-done), channel_id=1, source_target_pairs={{0,1},{1,0},{2,3},{3,2},{4,5},{5,4},{6,7},{7,6},{8,9},{9,8},{10,11... | collective-permute-start | bytes 786440 | tf_op jit(solution)/shard_map/ppermute | solution.py:214
  16.1 13.2 %copy-start.1 = (bf16[2,64,8,128]{3,2,1,0:T(8,128)(2,1)S(1)}, bf16[2,64,8,128]{3,2,1,0:T(8,128)(2,1)}, u32[]{:S(2)}) copy-start(bf16[2,64,8,128]{3,2,1,0:T(8,128)(2,1)} %param.9) | copy-start | bytes 786436
  16.1 13.2 %copy-start.2 = (bf16[2,64,64]{2,1,0:T(8,128)(2,1)S(1)}, bf16[2,64,64]{2,1,0:T(8,128)(2,1)}, u32[]{:S(2)}) copy-start(bf16[2,64,64]{2,1,0:T(8,128)(2,1)} %vert_ref.1) | copy-start | bytes 49156
  16.2 13.2 %copy-start.5 = (f32[8]{0:T(128)S(1)}, f32[8]{0:T(128)}, u32[]{:S(2)}) copy-start(f32[8]{0:T(128)} %param.16) | copy-start | bytes 100
  20.4 15.1 %collective-permute-start.3 = (bf16[2,64,8,128]{3,2,1,0:T(8,128)(2,1)S(1)}, bf16[2,64,8,128]{3,2,1,0:T(8,128)(2,1)S(1)}, u32[]{:S(2)}, u32[]{:S(2)}) collective-permute-start(bf16[2,64,8,128]{3,2,1,0:T(8,128)(2,1)S(1)} %bitcast.16), channel_id=1, source_target_pairs={{16,0},{32,16},{48,32},{64,48},{80,64},{96,80},{112,96},{128,112},... | collective-permute-start | bytes 786440 | tf_op jit(solution)/shard_map/ppermute | solution.py:239
  24.0 15.8 %collective-permute-start.2 = (bf16[2,64,8,128]{3,2,1,0:T(8,128)(2,1)S(1)}, bf16[2,64,8,128]{3,2,1,0:T(8,128)(2,1)S(1)}, u32[]{:S(2)}, u32[]{:S(2)}) collective-permute-start(bf16[2,64,8,128]{3,2,1,0:T(8,128)(2,1)S(1)} %bitcast.17), channel_id=1, source_target_pairs={{0,16},{16,32},{32,48},{48,64},{64,80},{80,96},{96,112},{112,128},... | collective-permute-start | bytes 786440 | tf_op jit(solution)/shard_map/ppermute | solution.py:238

commit v3 on v2

--- a/solution.py
+++ b/solution.py
@@ -1,3 +1,5 @@
+import functools
+
 import jax
 import jax.numpy as jnp
 from jax import lax
@@ -62,7 +64,7 @@
 
 
 def lon_kernel(
-    record_ref, own_hbm, rate_x_hbm, sum_ref, x_ref, own_ref, rate_x_ref, rate_ref, list_ref, hit_ref, spread_ref, sems
+    record_ref, own_hbm, rate_x_hbm, sum_ref, x_ref, own_ref, rate_x_ref, rate_ref, list_ref, sems
 ):
     copies = [
         pltpu.make_async_copy(rate_x_hbm, rate_x_ref, sems.at[0]),
@@ -114,22 +116,27 @@
             own_ref[c * ROWS : (c + 1) * ROWS], middle, preferred_element_type=F32
         )
 
-    def step(i, carry):
-        record = list_ref[:, pl.ds(pl.multiple_of(i * PARTS, PARTS), PARTS), :]
+    def add(start):
+        record = list_ref[:, pl.ds(pl.multiple_of(start, PARTS), PARTS), :]
         places = iota((ROWS, CX), 0) - ROWS // 2
         columns = (iota((CX, CX), 0) - CX // 2).astype(F32)
+        hits, spreads = [], []
         for part in range(PARTS):
-            at = slice(part * CX, (part + 1) * CX)
-            row = lambda f: record[f, part : part + 1]
-            hit_ref[:, at] = jnp.where(places == row(0).astype(I32), 1.0, 0.0).astype(BF16)
-            far = jnp.abs(columns - row(1))
+            place, column, first, second = (record[f, part : part + 1] for f in range(4))
+            hits.append(jnp.where(places == place.astype(I32), 1.0, 0.0).astype(BF16))
+            far = jnp.abs(columns - column)
             weight = jnp.where(far <= CX, jnp.exp(far * rate_ref[...]), 0.0)
-            for c in range(2):
-                spread_ref[c * CX : (c + 1) * CX, at] = (weight * row(2 + c)).astype(BF16)
-        sum_ref[...] += lax.dot_general(hit_ref[...], spread_ref[...], ACROSS, preferred_element_type=F32)
+            spreads.append(jnp.concatenate([weight * first, weight * second], axis=0).astype(BF16))
+        sum_ref[...] += lax.dot_general(
+            jnp.concatenate(hits, axis=1), jnp.concatenate(spreads, axis=1), ACROSS, preferred_element_type=F32
+        )
+
+    def step(i, carry):
+        add(2 * PARTS * i)
+        add(2 * PARTS * i + PARTS)
         return carry
 
-    lax.fori_loop(0, (used_rows + PARTS - 1) // PARTS, step, 0)
+    lax.fori_loop(0, (used_rows + 2 * PARTS - 1) // (2 * PARTS), step, 0)
 
 
 def dense_kernel(sum_ref, near_ref, far_ref, x_ref, out_ref):
@@ -159,25 +166,25 @@
             near = jnp.logical_and(near, band < bands - 1)
         weight = jnp.where(near, jnp.exp(-far.astype(F32) * rate / CY), 0.0)
         weights.append(jnp.concatenate([weight.astype(BF16).astype(F32)] * (ROWS // CX), axis=1))
+    even = band % 2 == 0
+    weights = [jnp.where(even, weights[2], weights[0]), weights[1], jnp.where(even, weights[0], weights[2])]
     for c in range(2):
         at = slice(c * ROWS, (c + 1) * ROWS)
         tall = jnp.dot(spread, vert_ref[c], preferred_element_type=F32).astype(BF16)
         wide = lax.dot_general(tall, spread, ACROSS, preferred_element_type=F32).reshape(LEV, CY, ROWS)
         for part in (0, 2):
             product = (wide * weights[part][None]).reshape(ROWS, ROWS)
-            y_ref[c, :, part // 2 * ROWS : (part // 2 + 1) * ROWS] = product.astype(BF16)
+            y_ref[part // 2, c] = product.astype(BF16)
         middle = (wide * weights[1][None]).reshape(ROWS, ROWS).astype(BF16)
         mixed = jnp.dot(middle, smooth_ref[at], preferred_element_type=F32)
         total_ref[at] = control_ref[at].astype(F32) + mixed
 
 
-def final_kernel(total_ref, lower_ref, upper_ref, y_ref, out_ref):
+def band_kernel(part, total_ref, band_ref, y_ref, out_ref):
     for c in range(2):
         at = slice(c * ROWS, (c + 1) * ROWS)
-        total = total_ref[at]
-        total += jnp.dot(y_ref[c, :, 0:ROWS], lower_ref[at], preferred_element_type=F32)
-        total += jnp.dot(y_ref[c, :, ROWS:], upper_ref[at], preferred_element_type=F32)
-        out_ref[at] = total.astype(BF16)
+        mixed = jnp.dot(y_ref[part, c], band_ref[at], preferred_element_type=F32)
+        out_ref[at] = (total_ref[at] + mixed).astype(out_ref.dtype)
 
 
 def call(kernel, out_shape, specs, scratch=(), flops=0, moved=0, limit=24):
@@ -223,8 +230,6 @@
             pltpu.VMEM((TILES, CX), F32),
             pltpu.VMEM((CX, CX), F32),
             pltpu.VMEM((4, TILES * PARTS, CX), F32),
-            pltpu.VMEM((ROWS, SLOTS), BF16),
-            pltpu.VMEM((2 * CX, SLOTS), BF16),
             pltpu.SemaphoreType.DMA((2,)),
         ],
         flops=2 * ROWS * 256 * TILES * SLOTS,
@@ -235,19 +240,24 @@
         total, inner.reshape(flat), outer.reshape(flat), x_weights
     )
     wide = smooth.reshape(shape)
-    lower = lax.ppermute(wide, "ry", [(i, i + 1) for i in range(bands - 1)])
-    upper = lax.ppermute(wide, "ry", [(i + 1, i) for i in range(bands - 1)])
+    inner = lax.ppermute(wide, "ry", [(i, i ^ 1) for i in range(bands)])
+    outer = lax.ppermute(wide, "ry", [(i, ((i + 1) ^ 1) - 1) for i in range(1, bands - 1)])
     total, y_weights = call(
         own_kernel,
-        [struct(flat, F32), struct((2, ROWS, 2 * ROWS), BF16)],
+        [struct(flat, F32), struct((2, 2, ROWS, ROWS), BF16)],
         [VMEM] * 4,
         flops=2 * 2 * ROWS * ROWS * CX * 2,
         moved=4000000,
     )(smooth, control.reshape(flat), rate_y.reshape(1, CY), vert)
-    out = call(final_kernel, struct(flat, BF16), [VMEM] * 4, flops=2 * 2 * ROWS * 2 * ROWS * CX, moved=4000000)(
-        total, lower.reshape(flat), upper.reshape(flat), y_weights
-    )
-    return out.reshape(shape)
+    for part, band, dtype in ((0, inner, F32), (1, outer, BF16)):
+        total = call(
+            functools.partial(band_kernel, part),
+            struct(flat, dtype),
+            [VMEM] * 3,
+            flops=2 * 2 * ROWS * ROWS * CX,
+            moved=2000000,
+        )(total, band.reshape(flat), y_weights)
+    return total.reshape(shape)
 
 
 def solution(mesh):

time: 41.7 us -> 39.5 us (0.947)
  the two profiles are of different devices: /device:TPU:121 before, /device:TPU:24 now
where the time goes in v3:
time: 39.5 us; the launch traced here: 38.7 us
  starting transfers between devices  20.7 us (52%)
  waiting for transfers between devices  8.23 us (21%)
  Pallas kernels  7.53 us (19%)
  between operations  0.78 us (2%)
  local copies, waits for them, and re-layouts  0.72 us (2%)
  other arithmetic  0.71 us (2%)
    ppermute x1, starting transfers between devices, body(): inner = lax.ppermute(wide, 'ry', [(i, i ^ 1) for i in range(bands)])  6.54 us
    all_to_all x1, starting transfers between devices, body(): records = lax.all_to_all(packed, 'rx', 0, 0, tiled=True)  5.78 us
    ppermute x1, waiting for transfers between devices, body(): lax.ppermute(wide, 'ry', [(i, (i + 1 ^ 1) - 1) for i in range(1, bands -...  5.33 us
    ppermute x1, starting transfers between devices, body(): lax.ppermute(held, 'rx', [(i, (i + 1 ^ 1) - 1) for i in range(1, tiles -...  4.33 us
    pallas_call x1, Pallas kernels, body(): call(lon_kernel, [struct((ROWS, 2 * CX), F32), struct((2 * CX, CX), BF16)...  3.29 us
    ppermute x1, waiting for transfers between devices, body(): inner = lax.ppermute(wide, 'ry', [(i, i ^ 1) for i in range(bands)])  2.72 us
    ppermute x1, starting transfers between devices, body(): lax.ppermute(wide, 'ry', [(i, (i + 1 ^ 1) - 1) for i in range(1, bands -...  2.16 us
    ppermute x1, starting transfers between devices, body(): inner = lax.ppermute(held, 'rx', [(i, i ^ 1) for i in range(tiles)])  1.92 us
  transfers between devices with their start and end apart: 5, of which 3 were waited for; matrix products, arithmetic and copies ran while one was open for 0% of the time, Pallas kernels for 12%

profile of v3, /device:TPU:24, one launch (start us, length us, event | category | flops | bytes accessed | tf_op | source)
XLA Modules:
  0.0 38.7 jit_solution(11801545193380006020)
XLA Ops:
  0.7 0.7 %pad_add_fusion.place_ref = s32[2,8,128]{2,1,0:T(8,128)S(1)} fusion(s32[1,8,128]{2,1,0:T(8,128)} %bitcast.24, s32[1,8,128]{2,1,0:T(8,128)} %bitcast.25), kind=kLoop, calls=%fused_computation | loop fusion | flops 2048 | bytes 16384 | tf_op jit(solution)/shard_map/stack | solution.py:209
  1.4 0.0 copy-start.3
  1.4 0.7 %copy-done.3 = f32[2,1024]{1,0:T(2,128)S(1)} copy-done((f32[2,1024]{1,0:T(2,128)S(1)}, f32[2,1024]{1,0:T(2,128)}, u32[]{:S(2)}) %copy-start.3) | copy-done | bytes 8216
  2.1 0.0 copy-start
  2.1 0.0 copy-start.4
  2.1 1.3 %shard_map.91 = bf16[16,32,128]{2,1,0:T(8,128)(2,1)} custom-call(s32[1,1]{1,0:T(1,128)} %bitcast.13.count_ref, s32[2,8,128]{2,1,0:T(8,128)S(1)} %pad_add_fusion.place_ref, f32[2,1024]{1,0:T(2,128)S(1)} %copy-done.3), custom_call_target="tpu_custom_call" | custom-call | flops 3000000000 | bytes 200000 | tf_op jit(solution)/shard_map/pallas_call | solution.py:210
  3.4 5.8 %all-to-all-start = ((bf16[16,32,128]{2,1,0:T(8,128)(2,1)}), bf16[16,32,128]{2,1,0:T(8,128)(2,1)S(1)}, u32[]{:S(2)}, u32[]{:S(2)}) async-start(bf16[16,32,128]{2,1,0:T(8,128)(2,1)} %shard_map.91), calls=%async_computation | async-start | bytes 262144 | tf_op jit(solution)/shard_map/all_to_all | solution.py:218
  9.2 0.0 copy-done
  9.2 4.3 %collective-permute-start.1 = (bf16[2,64,8,128]{3,2,1,0:T(8,128)(2,1)S(1)}, bf16[2,64,8,128]{3,2,1,0:T(8,128)(2,1)S(1)}, u32[]{:S(2)}, u32[]{:S(2)}) collective-permute-start(bf16[2,64,8,128]{3,2,1,0:T(8,128)(2,1)S(1)} %copy-done), channel_id=1, source_target_pairs={{1,2},{2,1},{3,4},{4,3},{5,6},{6,5},{7,8},{8,7},{9,10},{10,9},{11,... | collective-permute-start | bytes 786440 | tf_op jit(solution)/shard_map/ppermute | solution.py:222
  13.5 1.9 %collective-permute-start = (bf16[2,64,8,128]{3,2,1,0:T(8,128)(2,1)S(1)}, bf16[2,64,8,128]{3,2,1,0:T(8,128)(2,1)S(1)}, u32[]{:S(2)}, u32[]{:S(2)}) collective-permute-start(bf16[2,64,8,128]{3,2,1,0:T(8,128)(2,1)S(1)} %copy-done), channel_id=1, source_target_pairs={{0,1},{1,0},{2,3},{3,2},{4,5},{5,4},{6,7},{7,6},{8,9},{9,8},{10,11... | collective-permute-start | bytes 786440 | tf_op jit(solution)/shard_map/ppermute | solution.py:221
  15.4 0.0 all-to-all-done.record_ref
  15.5 0.0 copy-done.4
  15.5 0.0 copy-start.1
  15.5 0.0 copy-start.2
  15.5 0.0 copy-start.5
  15.5 3.3 %shard_map.92 = (f32[512,256]{1,0:T(8,128)S(1)}, bf16[256,128]{1,0:T(8,128)(2,1)S(1)}) custom-call(bf16[16,32,128]{2,1,0:T(8,128)(2,1)S(1)} %all-to-all-done.record_ref, bf16[1024,128]{1,0:T(8,128)(2,1)S(1)} %bitcast.20, f32[16,128]{1,0:T(8,128)S(1)} %bitcast.22), custom_call_target="tpu_custom_call" | custom-call | flops 4294967296 | bytes 1000000 | tf_op jit(solution)/shard_map/pallas_call | solution.py:224
  18.8 0.2 collective-permute-done.1
  19.0 0.0 collective-permute-done
  19.0 0.3 shard_map.93.smooth_ref
  19.3 6.5 %collective-permute-start.2 = (bf16[2,64,8,128]{3,2,1,0:T(8,128)(2,1)S(1)}, bf16[2,64,8,128]{3,2,1,0:T(8,128)(2,1)S(1)}, u32[]{:S(2)}, u32[]{:S(2)}) collective-permute-start(bf16[2,64,8,128]{3,2,1,0:T(8,128)(2,1)S(1)} %bitcast.15), channel_id=1, source_target_pairs={{0,16},{16,0},{32,48},{48,32},{64,80},{80,64},{96,112},{112,96},{1... | collective-permute-start | bytes 786440 | tf_op jit(solution)/shard_map/ppermute | solution.py:243
  25.8 2.2 %collective-permute-start.3 = (bf16[2,64,8,128]{3,2,1,0:T(8,128)(2,1)S(1)}, bf16[2,64,8,128]{3,2,1,0:T(8,128)(2,1)S(1)}, u32[]{:S(2)}, u32[]{:S(2)}) collective-permute-start(bf16[2,64,8,128]{3,2,1,0:T(8,128)(2,1)S(1)} %bitcast.16), channel_id=1, source_target_pairs={{16,32},{32,16},{48,64},{64,48},{80,96},{96,80},{112,128},{128,112... | collective-permute-start | bytes 786440 | tf_op jit(solution)/shard_map/ppermute | solution.py:244
  28.0 0.0 copy-done.1
  28.0 0.0 copy-done.2
  28.0 0.0 copy-done.5
  28.0 1.0 %shard_map.94 = (f32[1024,128]{1,0:T(8,128)S(1)}, bf16[2,2,512,512]{3,2,1,0:T(8,128)(2,1)S(1)}) custom-call(bf16[1024,128]{1,0:T(8,128)(2,1)S(1)} %shard_map.93.smooth_ref, bf16[1024,128]{1,0:T(8,128)(2,1)S(1)} %bitcast.21, f32[1,8]{1,0:T(1,128)S(1)} %bitcast.23, bf16[2,64,64]{2,1,0:T(8,128)(2,1)S(1)} %copy-done.2), custom_call_target="tpu_custom_call" | custom-call | flops 268435456 | bytes 4000000 | tf_op jit(solution)/shard_map/pallas_call | solution.py:245
  29.1 2.7 %collective-permute-done.2 = bf16[2,64,8,128]{3,2,1,0:T(8,128)(2,1)S(1)} collective-permute-done((bf16[2,64,8,128]{3,2,1,0:T(8,128)(2,1)S(1)}, bf16[2,64,8,128]{3,2,1,0:T(8,128)(2,1)S(1)}, u32[]{:S(2)}, u32[]{:S(2)}) %collective-permute-start.2) | collective-permute-done | bytes 262176 | tf_op jit(solution)/shard_map/ppermute | solution.py:243
  31.8 0.4 %shard_map.95.total_ref = f32[1024,128]{1,0:T(8,128)S(1)} custom-call(f32[1024,128]{1,0:T(8,128)S(1)} %get-tuple-element.13.total_ref, bf16[1024,128]{1,0:T(8,128)(2,1)S(1)} %bitcast.19, bf16[2,2,512,512]{3,2,1,0:T(8,128)(2,1)S(1)} %get-tuple-element.14.y_ref), custom_call_target="tpu_custom_call" | custom-call | flops 134217728 | bytes 2000000 | tf_op jit(solution)/shard_map/pallas_call | solution.py:253
  32.2 5.3 %collective-permute-done.3 = bf16[2,64,8,128]{3,2,1,0:T(8,128)(2,1)S(1)} collective-permute-done((bf16[2,64,8,128]{3,2,1,0:T(8,128)(2,1)S(1)}, bf16[2,64,8,128]{3,2,1,0:T(8,128)(2,1)S(1)}, u32[]{:S(2)}, u32[]{:S(2)}) %collective-permute-start.3) | collective-permute-done | bytes 262176 | tf_op jit(solution)/shard_map/ppermute | solution.py:244
  37.6 1.2 %shard_map.96 = bf16[1024,128]{1,0:T(8,128)(2,1)} custom-call(f32[1024,128]{1,0:T(8,128)S(1)} %shard_map.95.total_ref, bf16[1024,128]{1,0:T(8,128)(2,1)S(1)} %bitcast.14, bf16[2,2,512,512]{3,2,1,0:T(8,128)(2,1)S(1)} %get-tuple-element.14.y_ref), custom_call_target="tpu_custom_call" | custom-call | flops 134217728 | bytes 2000000 | tf_op jit(solution)/shard_map/pallas_call | solution.py:253
Async XLA Ops:
  1.4 0.7 %copy-start.3 = (f32[2,1024]{1,0:T(2,128)S(1)}, f32[2,1024]{1,0:T(2,128)}, u32[]{:S(2)}) copy-start(f32[2,1024]{1,0:T(2,128)} %value_ref.1) | copy-start | bytes 24580
  2.1 7.1 %copy-start = (bf16[2,64,8,128]{3,2,1,0:T(8,128)(2,1)S(1)}, bf16[2,64,8,128]{3,2,1,0:T(8,128)(2,1)}, u32[]{:S(2)}) copy-start(bf16[2,64,8,128]{3,2,1,0:T(8,128)(2,1)} %param.10) | copy-start | bytes 786436
  2.1 13.4 %copy-start.4 = (f32[2048]{0:T(1024)S(1)}, f32[2048]{0:T(1024)}, u32[]{:S(2)}) copy-start(f32[2048]{0:T(1024)} %param.15) | copy-start | bytes 24580
  3.4 12.1 %all-to-all-start = ((bf16[16,32,128]{2,1,0:T(8,128)(2,1)}), bf16[16,32,128]{2,1,0:T(8,128)(2,1)S(1)}, u32[]{:S(2)}, u32[]{:S(2)}) async-start(bf16[16,32,128]{2,1,0:T(8,128)(2,1)} %shard_map.91), calls=%async_computation | async-start | bytes 262144 | tf_op jit(solution)/shard_map/all_to_all | solution.py:218
  9.2 9.8 %collective-permute-start.1 = (bf16[2,64,8,128]{3,2,1,0:T(8,128)(2,1)S(1)}, bf16[2,64,8,128]{3,2,1,0:T(8,128)(2,1)S(1)}, u32[]{:S(2)}, u32[]{:S(2)}) collective-permute-start(bf16[2,64,8,128]{3,2,1,0:T(8,128)(2,1)S(1)} %copy-done), channel_id=1, source_target_pairs={{1,2},{2,1},{3,4},{4,3},{5,6},{6,5},{7,8},{8,7},{9,10},{10,9},{11,... | collective-permute-start | bytes 786440 | tf_op jit(solution)/shard_map/ppermute | solution.py:222
  13.5 5.5 %collective-permute-start = (bf16[2,64,8,128]{3,2,1,0:T(8,128)(2,1)S(1)}, bf16[2,64,8,128]{3,2,1,0:T(8,128)(2,1)S(1)}, u32[]{:S(2)}, u32[]{:S(2)}) collective-permute-start(bf16[2,64,8,128]{3,2,1,0:T(8,128)(2,1)S(1)} %copy-done), channel_id=1, source_target_pairs={{0,1},{1,0},{2,3},{3,2},{4,5},{5,4},{6,7},{7,6},{8,9},{9,8},{10,11... | collective-permute-start | bytes 786440 | tf_op jit(solution)/shard_map/ppermute | solution.py:221
  15.5 12.5 %copy-start.1 = (bf16[2,64,8,128]{3,2,1,0:T(8,128)(2,1)S(1)}, bf16[2,64,8,128]{3,2,1,0:T(8,128)(2,1)}, u32[]{:S(2)}) copy-start(bf16[2,64,8,128]{3,2,1,0:T(8,128)(2,1)} %param.9) | copy-start | bytes 786436
  15.5 12.5 %copy-start.2 = (bf16[2,64,64]{2,1,0:T(8,128)(2,1)S(1)}, bf16[2,64,64]{2,1,0:T(8,128)(2,1)}, u32[]{:S(2)}) copy-start(bf16[2,64,64]{2,1,0:T(8,128)(2,1)} %vert_ref.1) | copy-start | bytes 49156
  15.5 12.5 %copy-start.5 = (f32[8]{0:T(128)S(1)}, f32[8]{0:T(128)}, u32[]{:S(2)}) copy-start(f32[8]{0:T(128)} %param.16) | copy-start | bytes 100
  19.3 12.5 %collective-permute-start.2 = (bf16[2,64,8,128]{3,2,1,0:T(8,128)(2,1)S(1)}, bf16[2,64,8,128]{3,2,1,0:T(8,128)(2,1)S(1)}, u32[]{:S(2)}, u32[]{:S(2)}) collective-permute-start(bf16[2,64,8,128]{3,2,1,0:T(8,128)(2,1)S(1)} %bitcast.15), channel_id=1, source_target_pairs={{0,16},{16,0},{32,48},{48,32},{64,80},{80,64},{96,112},{112,96},{1... | collective-permute-start | bytes 786440 | tf_op jit(solution)/shard_map/ppermute | solution.py:243
  25.8 11.7 %collective-permute-start.3 = (bf16[2,64,8,128]{3,2,1,0:T(8,128)(2,1)S(1)}, bf16[2,64,8,128]{3,2,1,0:T(8,128)(2,1)S(1)}, u32[]{:S(2)}, u32[]{:S(2)}) collective-permute-start(bf16[2,64,8,128]{3,2,1,0:T(8,128)(2,1)S(1)} %bitcast.16), channel_id=1, source_target_pairs={{16,32},{32,16},{48,64},{64,48},{80,96},{96,80},{112,128},{128,112... | collective-permute-start | bytes 786440 | tf_op jit(solution)/shard_map/ppermute | solution.py:244

commit v4 on v3

--- a/solution.py
+++ b/solution.py
@@ -26,19 +26,27 @@
     return lax.broadcasted_iota(I32, shape, axis)
 
 
-def pack_kernel(count_ref, place_ref, value_ref, out_ref, field_ref, lane_ref):
+def pack_kernel(
+    count_ref, tile_hbm, cell_hbm, value_hbm, out_ref, tiles, cells, values, field_ref, lane_ref, sems
+):
+    pairs = ((tile_hbm, tiles), (cell_hbm, cells), (value_hbm, values))
+    copies = [pltpu.make_async_copy(a, b, sems.at[i]) for i, (a, b) in enumerate(pairs)]
+    for copy in copies:
+        copy.start()
     before = (iota((CX, CX), 0) <= iota((CX, CX), 1)).astype(F32).astype(BF16)
     above = (iota((CX, CX), 0) > iota((CX, CX), 1)).astype(F32).astype(BF16)
     slot = iota((PARTS, CX), 0) * CX + iota((PARTS, CX), 1)
-    used = slot < count_ref[...]
-    tile = jnp.where(used, place_ref[0], -1)
-    cell = place_ref[1]
+    for copy in copies:
+        copy.wait()
+    used = slot < count_ref[0]
+    tile = jnp.where(used, tiles[...], -1)
+    cell = cells[...]
     fields = [
         (cell // CX - ROWS // 2).astype(F32),
         (tile + 1).astype(F32),
         (cell % CX - CX // 2).astype(F32),
-        value_ref[0:1].reshape(PARTS, CX),
-        value_ref[1:2].reshape(PARTS, CX),
+        values[0:1].reshape(PARTS, CX),
+        values[1:2].reshape(PARTS, CX),
     ]
 
     named = jnp.concatenate([jnp.where(tile == t, 1.0, 0.0) for t in range(TILES)], axis=0)
@@ -206,15 +214,22 @@
     bands, tiles = lax.axis_size("ry"), lax.axis_size("rx")
     struct = jax.ShapeDtypeStruct
 
-    places = jnp.stack([obs_tile.reshape(PARTS, CX), obs_cell.reshape(PARTS, CX)])
+    inputs = (obs_count, obs_tile.reshape(PARTS, CX), obs_cell.reshape(PARTS, CX), obs_value)
     packed = call(
         pack_kernel,
         struct((TILES, 4 * PARTS, CX), BF16),
-        [VMEM] * 3,
-        [pltpu.VMEM((5 * PARTS, SLOTS), BF16), pltpu.VMEM((CX, SLOTS), BF16)],
+        [pl.BlockSpec(memory_space=pltpu.SMEM)] + [HBM] * 3,
+        [
+            pltpu.VMEM((PARTS, CX), I32),
+            pltpu.VMEM((PARTS, CX), I32),
+            pltpu.VMEM((2, SLOTS), F32),
+            pltpu.VMEM((5 * PARTS, SLOTS), BF16),
+            pltpu.VMEM((CX, SLOTS), BF16),
+            pltpu.SemaphoreType.DMA((3,)),
+        ],
         flops=3 * 10**9,
         moved=200000,
-    )(obs_count.reshape(1, 1), places, obs_value)
+    )(inputs[0], *(pltpu.with_memory_space_constraint(x, pltpu.HBM) for x in inputs[1:]))
     records = lax.all_to_all(packed, "rx", 0, 0, tiled=True)
 
     held, _ = lax.optimization_barrier((forcing, packed))

time: 39.5 us -> 38.6 us (0.977)
  waiting for transfers between devices: 8.23 us -> 9.07 us
  other arithmetic: 0.71 us -> 0 us
  local copies, waits for them, and re-layouts: 0.72 us -> 0.03 us
    ppermute x1, waiting for transfers between devices: 0.17 us -> 0.99 us  [body(): lax.ppermute(held, 'rx', [(i, (i + 1 ^ 1) - 1) for i in range(1, tiles -...]
    pallas_call x1, Pallas kernels: 3.29 us -> 2.48 us  [body(): call(lon_kernel, [struct((ROWS, 2 * CX), F32), struct((2 * CX, CX), BF16)...]
    pallas_call x1, Pallas kernels: 1.33 us -> 2.07 us  [body(): call(pack_kernel, struct((TILES, 4 * PARTS, CX), BF16), [pl.BlockSpec(mem...]
    another operation x1 -> x0, other arithmetic: 0.71 us -> none  [body(): jnp.stack([obs_tile.reshape(PARTS, CX), obs_cell.reshape(PARTS, CX)])]
    unnamed x12 -> x10, local copies, waits for them, and re-layouts: 0.72 us -> 0.03 us
  transfers between devices with their start and end apart: 5 -> 5, of which waited for: 3 -> 3; matrix products, arithmetic and copies ran while one was open for 0% -> 0% of each run, Pallas kernels for 12% -> 10%
where the time goes in v4:
time: 38.6 us; the launch traced here: 38.1 us
  starting transfers between devices  20.7 us (54%)
  waiting for transfers between devices  9.07 us (23%)
  Pallas kernels  7.44 us (19%)
  between operations  0.8 us (2%)
    ppermute x1, starting transfers between devices, body(): inner = lax.ppermute(wide, 'ry', [(i, i ^ 1) for i in range(bands)])  6.54 us
    all_to_all x1, starting transfers between devices, body(): records = lax.all_to_all(packed, 'rx', 0, 0, tiled=True)  5.79 us
    ppermute x1, waiting for transfers between devices, body(): lax.ppermute(wide, 'ry', [(i, (i + 1 ^ 1) - 1) for i in range(1, bands -...  5.33 us
    ppermute x1, starting transfers between devices, body(): lax.ppermute(held, 'rx', [(i, (i + 1 ^ 1) - 1) for i in range(1, tiles -...  4.33 us
    ppermute x1, waiting for transfers between devices, body(): inner = lax.ppermute(wide, 'ry', [(i, i ^ 1) for i in range(bands)])  2.74 us
    pallas_call x1, Pallas kernels, body(): call(lon_kernel, [struct((ROWS, 2 * CX), F32), struct((2 * CX, CX), BF16)...  2.48 us
    ppermute x1, starting transfers between devices, body(): lax.ppermute(wide, 'ry', [(i, (i + 1 ^ 1) - 1) for i in range(1, bands -...  2.17 us
    pallas_call x1, Pallas kernels, body(): call(pack_kernel, struct((TILES, 4 * PARTS, CX), BF16), [pl.BlockSpec(mem...  2.07 us
  transfers between devices with their start and end apart: 5, of which 3 were waited for; matrix products, arithmetic and copies ran while one was open for 0% of the time, Pallas kernels for 10%

profile of v4, /device:TPU:24, one launch (start us, length us, event | category | flops | bytes accessed | tf_op | source)
XLA Modules:
  0.0 38.1 jit_solution(17956463604984210244)
XLA Ops:
  0.7 0.0 copy-start
  0.7 0.0 copy-start.3
  0.7 2.1 %shard_map.91 = bf16[16,32,128]{2,1,0:T(8,128)(2,1)} custom-call(s32[1]{0:T(128)S(6)} %copy.10.count_ref, s32[8,128]{1,0:T(8,128)} %bitcast.22, s32[8,128]{1,0:T(8,128)} %bitcast.23, f32[2,1024]{1,0:T(2,128)} %value_hbm.1), custom_call_target="tpu_custom_call" | custom-call | flops 3000000000 | bytes 200000 | tf_op jit(solution)/shard_map/pallas_call | solution.py:218
  2.7 5.8 %all-to-all-start = ((bf16[16,32,128]{2,1,0:T(8,128)(2,1)}), bf16[16,32,128]{2,1,0:T(8,128)(2,1)S(1)}, u32[]{:S(2)}, u32[]{:S(2)}) async-start(bf16[16,32,128]{2,1,0:T(8,128)(2,1)} %shard_map.91), calls=%async_computation | async-start | bytes 262144 | tf_op jit(solution)/shard_map/all_to_all | solution.py:233
  8.5 0.0 copy-done
  8.5 4.3 %collective-permute-start.1 = (bf16[2,64,8,128]{3,2,1,0:T(8,128)(2,1)S(1)}, bf16[2,64,8,128]{3,2,1,0:T(8,128)(2,1)S(1)}, u32[]{:S(2)}, u32[]{:S(2)}) collective-permute-start(bf16[2,64,8,128]{3,2,1,0:T(8,128)(2,1)S(1)} %copy-done), channel_id=1, source_target_pairs={{1,2},{2,1},{3,4},{4,3},{5,6},{6,5},{7,8},{8,7},{9,10},{10,9},{11,... | collective-permute-start | bytes 786440 | tf_op jit(solution)/shard_map/ppermute | solution.py:237
  12.9 1.9 %collective-permute-start = (bf16[2,64,8,128]{3,2,1,0:T(8,128)(2,1)S(1)}, bf16[2,64,8,128]{3,2,1,0:T(8,128)(2,1)S(1)}, u32[]{:S(2)}, u32[]{:S(2)}) collective-permute-start(bf16[2,64,8,128]{3,2,1,0:T(8,128)(2,1)S(1)} %copy-done), channel_id=1, source_target_pairs={{0,1},{1,0},{2,3},{3,2},{4,5},{5,4},{6,7},{7,6},{8,9},{9,8},{10,11... | collective-permute-start | bytes 786440 | tf_op jit(solution)/shard_map/ppermute | solution.py:236
  14.8 0.0 all-to-all-done.record_ref
  14.8 0.0 copy-done.3
  14.8 0.0 copy-start.1
  14.8 0.0 copy-start.2
  14.9 0.0 copy-start.4
  14.9 2.5 %shard_map.92 = (f32[512,256]{1,0:T(8,128)S(1)}, bf16[256,128]{1,0:T(8,128)(2,1)S(1)}) custom-call(bf16[16,32,128]{2,1,0:T(8,128)(2,1)S(1)} %all-to-all-done.record_ref, bf16[1024,128]{1,0:T(8,128)(2,1)S(1)} %bitcast.18, f32[16,128]{1,0:T(8,128)S(1)} %bitcast.20), custom_call_target="tpu_custom_call" | custom-call | flops 4294967296 | bytes 1000000 | tf_op jit(solution)/shard_map/pallas_call | solution.py:239
  17.4 1.0 %collective-permute-done.1 = bf16[2,64,8,128]{3,2,1,0:T(8,128)(2,1)S(1)} collective-permute-done((bf16[2,64,8,128]{3,2,1,0:T(8,128)(2,1)S(1)}, bf16[2,64,8,128]{3,2,1,0:T(8,128)(2,1)S(1)}, u32[]{:S(2)}, u32[]{:S(2)}) %collective-permute-start.1) | collective-permute-done | bytes 262176 | tf_op jit(solution)/shard_map/ppermute | solution.py:237
  18.3 0.0 collective-permute-done
  18.3 0.3 shard_map.93.smooth_ref
  18.6 6.5 %collective-permute-start.2 = (bf16[2,64,8,128]{3,2,1,0:T(8,128)(2,1)S(1)}, bf16[2,64,8,128]{3,2,1,0:T(8,128)(2,1)S(1)}, u32[]{:S(2)}, u32[]{:S(2)}) collective-permute-start(bf16[2,64,8,128]{3,2,1,0:T(8,128)(2,1)S(1)} %bitcast.13), channel_id=1, source_target_pairs={{0,16},{16,0},{32,48},{48,32},{64,80},{80,64},{96,112},{112,96},{1... | collective-permute-start | bytes 786440 | tf_op jit(solution)/shard_map/ppermute | solution.py:258
  25.2 2.2 %collective-permute-start.3 = (bf16[2,64,8,128]{3,2,1,0:T(8,128)(2,1)S(1)}, bf16[2,64,8,128]{3,2,1,0:T(8,128)(2,1)S(1)}, u32[]{:S(2)}, u32[]{:S(2)}) collective-permute-start(bf16[2,64,8,128]{3,2,1,0:T(8,128)(2,1)S(1)} %bitcast.14), channel_id=1, source_target_pairs={{16,32},{32,16},{48,64},{64,48},{80,96},{96,80},{112,128},{128,112... | collective-permute-start | bytes 786440 | tf_op jit(solution)/shard_map/ppermute | solution.py:259
  27.3 0.0 copy-done.1
  27.4 0.0 copy-done.2
  27.4 0.0 copy-done.4
  27.4 1.0 %shard_map.94 = (f32[1024,128]{1,0:T(8,128)S(1)}, bf16[2,2,512,512]{3,2,1,0:T(8,128)(2,1)S(1)}) custom-call(bf16[1024,128]{1,0:T(8,128)(2,1)S(1)} %shard_map.93.smooth_ref, bf16[1024,128]{1,0:T(8,128)(2,1)S(1)} %bitcast.19, f32[1,8]{1,0:T(1,128)S(1)} %bitcast.21, bf16[2,64,64]{2,1,0:T(8,128)(2,1)S(1)} %copy-done.2), custom_call_target="tpu_custom_call" | custom-call | flops 268435456 | bytes 4000000 | tf_op jit(solution)/shard_map/pallas_call | solution.py:260
  28.4 2.7 %collective-permute-done.2 = bf16[2,64,8,128]{3,2,1,0:T(8,128)(2,1)S(1)} collective-permute-done((bf16[2,64,8,128]{3,2,1,0:T(8,128)(2,1)S(1)}, bf16[2,64,8,128]{3,2,1,0:T(8,128)(2,1)S(1)}, u32[]{:S(2)}, u32[]{:S(2)}) %collective-permute-start.2) | collective-permute-done | bytes 262176 | tf_op jit(solution)/shard_map/ppermute | solution.py:258
  31.2 0.4 %shard_map.95.total_ref = f32[1024,128]{1,0:T(8,128)S(1)} custom-call(f32[1024,128]{1,0:T(8,128)S(1)} %get-tuple-element.13.total_ref, bf16[1024,128]{1,0:T(8,128)(2,1)S(1)} %bitcast.17, bf16[2,2,512,512]{3,2,1,0:T(8,128)(2,1)S(1)} %get-tuple-element.14.y_ref), custom_call_target="tpu_custom_call" | custom-call | flops 134217728 | bytes 2000000 | tf_op jit(solution)/shard_map/pallas_call | solution.py:268
  31.6 5.3 %collective-permute-done.3 = bf16[2,64,8,128]{3,2,1,0:T(8,128)(2,1)S(1)} collective-permute-done((bf16[2,64,8,128]{3,2,1,0:T(8,128)(2,1)S(1)}, bf16[2,64,8,128]{3,2,1,0:T(8,128)(2,1)S(1)}, u32[]{:S(2)}, u32[]{:S(2)}) %collective-permute-start.3) | collective-permute-done | bytes 262176 | tf_op jit(solution)/shard_map/ppermute | solution.py:259
  36.9 1.2 %shard_map.96 = bf16[1024,128]{1,0:T(8,128)(2,1)} custom-call(f32[1024,128]{1,0:T(8,128)S(1)} %shard_map.95.total_ref, bf16[1024,128]{1,0:T(8,128)(2,1)S(1)} %bitcast.12, bf16[2,2,512,512]{3,2,1,0:T(8,128)(2,1)S(1)} %get-tuple-element.14.y_ref), custom_call_target="tpu_custom_call" | custom-call | flops 134217728 | bytes 2000000 | tf_op jit(solution)/shard_map/pallas_call | solution.py:268
Async XLA Ops:
  0.7 7.9 %copy-start = (bf16[2,64,8,128]{3,2,1,0:T(8,128)(2,1)S(1)}, bf16[2,64,8,128]{3,2,1,0:T(8,128)(2,1)}, u32[]{:S(2)}) copy-start(bf16[2,64,8,128]{3,2,1,0:T(8,128)(2,1)} %param.10) | copy-start | bytes 786436
  0.7 14.2 %copy-start.3 = (f32[2048]{0:T(1024)S(1)}, f32[2048]{0:T(1024)}, u32[]{:S(2)}) copy-start(f32[2048]{0:T(1024)} %param.15) | copy-start | bytes 24580
  2.7 12.1 %all-to-all-start = ((bf16[16,32,128]{2,1,0:T(8,128)(2,1)}), bf16[16,32,128]{2,1,0:T(8,128)(2,1)S(1)}, u32[]{:S(2)}, u32[]{:S(2)}) async-start(bf16[16,32,128]{2,1,0:T(8,128)(2,1)} %shard_map.91), calls=%async_computation | async-start | bytes 262144 | tf_op jit(solution)/shard_map/all_to_all | solution.py:233
  8.5 9.8 %collective-permute-start.1 = (bf16[2,64,8,128]{3,2,1,0:T(8,128)(2,1)S(1)}, bf16[2,64,8,128]{3,2,1,0:T(8,128)(2,1)S(1)}, u32[]{:S(2)}, u32[]{:S(2)}) collective-permute-start(bf16[2,64,8,128]{3,2,1,0:T(8,128)(2,1)S(1)} %copy-done), channel_id=1, source_target_pairs={{1,2},{2,1},{3,4},{4,3},{5,6},{6,5},{7,8},{8,7},{9,10},{10,9},{11,... | collective-permute-start | bytes 786440 | tf_op jit(solution)/shard_map/ppermute | solution.py:237
  12.9 5.5 %collective-permute-start = (bf16[2,64,8,128]{3,2,1,0:T(8,128)(2,1)S(1)}, bf16[2,64,8,128]{3,2,1,0:T(8,128)(2,1)S(1)}, u32[]{:S(2)}, u32[]{:S(2)}) collective-permute-start(bf16[2,64,8,128]{3,2,1,0:T(8,128)(2,1)S(1)} %copy-done), channel_id=1, source_target_pairs={{0,1},{1,0},{2,3},{3,2},{4,5},{5,4},{6,7},{7,6},{8,9},{9,8},{10,11... | collective-permute-start | bytes 786440 | tf_op jit(solution)/shard_map/ppermute | solution.py:236
  14.8 12.5 %copy-start.1 = (bf16[2,64,8,128]{3,2,1,0:T(8,128)(2,1)S(1)}, bf16[2,64,8,128]{3,2,1,0:T(8,128)(2,1)}, u32[]{:S(2)}) copy-start(bf16[2,64,8,128]{3,2,1,0:T(8,128)(2,1)} %param.9) | copy-start | bytes 786436
  14.8 12.5 %copy-start.2 = (bf16[2,64,64]{2,1,0:T(8,128)(2,1)S(1)}, bf16[2,64,64]{2,1,0:T(8,128)(2,1)}, u32[]{:S(2)}) copy-start(bf16[2,64,64]{2,1,0:T(8,128)(2,1)} %vert_ref.1) | copy-start | bytes 49156
  14.9 12.5 %copy-start.4 = (f32[8]{0:T(128)S(1)}, f32[8]{0:T(128)}, u32[]{:S(2)}) copy-start(f32[8]{0:T(128)} %param.16) | copy-start | bytes 100
  18.6 12.5 %collective-permute-start.2 = (bf16[2,64,8,128]{3,2,1,0:T(8,128)(2,1)S(1)}, bf16[2,64,8,128]{3,2,1,0:T(8,128)(2,1)S(1)}, u32[]{:S(2)}, u32[]{:S(2)}) collective-permute-start(bf16[2,64,8,128]{3,2,1,0:T(8,128)(2,1)S(1)} %bitcast.13), channel_id=1, source_target_pairs={{0,16},{16,0},{32,48},{48,32},{64,80},{80,64},{96,112},{112,96},{1... | collective-permute-start | bytes 786440 | tf_op jit(solution)/shard_map/ppermute | solution.py:258
  25.2 11.8 %collective-permute-start.3 = (bf16[2,64,8,128]{3,2,1,0:T(8,128)(2,1)S(1)}, bf16[2,64,8,128]{3,2,1,0:T(8,128)(2,1)S(1)}, u32[]{:S(2)}, u32[]{:S(2)}) collective-permute-start(bf16[2,64,8,128]{3,2,1,0:T(8,128)(2,1)S(1)} %bitcast.14), channel_id=1, source_target_pairs={{16,32},{32,16},{48,64},{64,48},{80,96},{96,80},{112,128},{128,112... | collective-permute-start | bytes 786440 | tf_op jit(solution)/shard_map/ppermute | solution.py:259

commit v5 on v4

--- a/solution.py
+++ b/solution.py
@@ -27,13 +27,14 @@
 
 
 def pack_kernel(
-    count_ref, tile_hbm, cell_hbm, value_hbm, out_ref, tiles, cells, values, field_ref, lane_ref, sems
+    count_ref, tile_hbm, cell_hbm, value_hbm, out_ref, tiles, cells, values, sems
 ):
     pairs = ((tile_hbm, tiles), (cell_hbm, cells), (value_hbm, values))
     copies = [pltpu.make_async_copy(a, b, sems.at[i]) for i, (a, b) in enumerate(pairs)]
     for copy in copies:
         copy.start()
-    before = (iota((CX, CX), 0) <= iota((CX, CX), 1)).astype(F32).astype(BF16)
+    before = (iota((CX, CX), 0) <= iota((CX, CX), 1)).astype(F32)
+    before = jnp.concatenate([before, jnp.ones((CX, CX), F32)], axis=0).astype(BF16)
     above = (iota((CX, CX), 0) > iota((CX, CX), 1)).astype(F32).astype(BF16)
     slot = iota((PARTS, CX), 0) * CX + iota((PARTS, CX), 1)
     for copy in copies:
@@ -50,21 +51,22 @@
     ]
 
     named = jnp.concatenate([jnp.where(tile == t, 1.0, 0.0) for t in range(TILES)], axis=0)
-    within = jnp.dot(named.astype(BF16), before, preferred_element_type=F32)
-    counts = jnp.broadcast_to(within[:, CX - 1 :], (CX, CX)).astype(BF16)
-    rank = named * (within + jnp.dot(above, counts, preferred_element_type=F32) - 1.0)
-    rank = jnp.sum(rank.reshape(TILES, PARTS, CX), axis=0)
+    both = named.astype(BF16)
+    lower = jnp.dot(above, both, preferred_element_type=F32).astype(BF16)
+    rank = jnp.dot(jnp.concatenate([both, lower], axis=1), before, preferred_element_type=F32)
+    rank = jnp.sum((named * (rank - 1.0)).reshape(TILES, PARTS, CX), axis=0)
     rank = jnp.where(used, rank, float(SLOTS)).astype(I32)
 
     row, lane = rank // CX, rank % CX
+    picked, lanes = [], []
     for part in range(PARTS):
-        at = slice(part * CX, (part + 1) * CX)
         here = iota((PARTS, CX), 0) == row[part : part + 1]
-        for i, field in enumerate(fields):
-            picked = jnp.where(here, field[part : part + 1], 0.0)
-            field_ref[i * PARTS : (i + 1) * PARTS, at] = picked.astype(BF16)
-        lane_ref[:, at] = jnp.where(iota((CX, CX), 0) == lane[part : part + 1], 1.0, 0.0).astype(BF16)
-    ordered = lax.dot_general(field_ref[...], lane_ref[...], ACROSS, preferred_element_type=F32)
+        rows = [jnp.where(here, field[part : part + 1], 0.0) for field in fields]
+        picked.append(jnp.concatenate(rows, axis=0).astype(BF16))
+        lanes.append(jnp.where(iota((CX, CX), 0) == lane[part : part + 1], 1.0, 0.0).astype(BF16))
+    ordered = lax.dot_general(
+        jnp.concatenate(picked, axis=1), jnp.concatenate(lanes, axis=1), ACROSS, preferred_element_type=F32
+    )
     place, named, column, first, second = (ordered[i * PARTS : (i + 1) * PARTS] for i in range(5))
     column = jnp.where(named > 0.0, (named - 1.0) * CX + column, 4.0 * TILES * CX)
     for t in range(TILES):
@@ -82,8 +84,9 @@
         copy.start()
 
     rows = TILES * PARTS
-    field = lambda f: record_ref[:, f * PARTS : (f + 1) * PARTS, :].reshape(rows, CX)
-    column = field(1).astype(F32)
+    record = record_ref[...].astype(F32)
+    field = lambda f: record[:, f * PARTS : (f + 1) * PARTS, :].reshape(rows, CX)
+    column = field(1)
     reached = jnp.logical_and(column >= -1.5 * CX, column < 1.5 * CX)
     some = jnp.max(jnp.where(reached, 1.0, 0.0), axis=1, keepdims=True)
     some = jnp.broadcast_to(some, (rows, CX)).astype(BF16)
@@ -96,7 +99,7 @@
     moved = jnp.logical_and(under == target_row, upto == target_row + 1.0)
     moved = jnp.where(moved, 1.0, 0.0).astype(BF16)
     for f in range(4):
-        list_ref[f] = jnp.dot(moved, field(f), preferred_element_type=F32)
+        list_ref[f] = jnp.dot(moved, field(f).astype(BF16), preferred_element_type=F32)
     used_rows = jnp.max(upto).astype(I32)
 
     tile, tiles = lax.axis_index("rx"), lax.axis_size("rx")
@@ -195,7 +198,7 @@
         out_ref[at] = (total_ref[at] + mixed).astype(out_ref.dtype)
 
 
-def call(kernel, out_shape, specs, scratch=(), flops=0, moved=0, limit=24):
+def call(kernel, out_shape, specs, scratch=(), flops=0, moved=0):
     many = isinstance(out_shape, (list, tuple))
     return pl.pallas_call(
         kernel,
@@ -204,7 +207,7 @@
         out_specs=[VMEM] * len(out_shape) if many else VMEM,
         scratch_shapes=list(scratch),
         cost_estimate=pl.CostEstimate(flops=flops, bytes_accessed=moved, transcendentals=0),
-        compiler_params=pltpu.CompilerParams(vmem_limit_bytes=limit * 2**20),
+        compiler_params=pltpu.CompilerParams(vmem_limit_bytes=24 * 2**20),
     )
 
 
@@ -223,8 +226,6 @@
             pltpu.VMEM((PARTS, CX), I32),
             pltpu.VMEM((PARTS, CX), I32),
             pltpu.VMEM((2, SLOTS), F32),
-            pltpu.VMEM((5 * PARTS, SLOTS), BF16),
-            pltpu.VMEM((CX, SLOTS), BF16),
             pltpu.SemaphoreType.DMA((3,)),
         ],
         flops=3 * 10**9,

time: 38.6 us -> 38.7 us (level)
  no operation moved by 1% of the time
where the time goes in v5:
time: 38.7 us; the launch traced here: 38 us
  starting transfers between devices  20.8 us (54%)
  waiting for transfers between devices  9.04 us (23%)
  Pallas kernels  7.34 us (19%)
  between operations  0.8 us (2%)
    ppermute x1, starting transfers between devices, body(): inner = lax.ppermute(wide, 'ry', [(i, i ^ 1) for i in range(bands)])  6.54 us
    all_to_all x1, starting transfers between devices, body(): records = lax.all_to_all(packed, 'rx', 0, 0, tiled=True)  5.79 us
    ppermute x1, waiting for transfers between devices, body(): lax.ppermute(wide, 'ry', [(i, (i + 1 ^ 1) - 1) for i in range(1, bands -...  5.33 us
    ppermute x1, starting transfers between devices, body(): lax.ppermute(held, 'rx', [(i, (i + 1 ^ 1) - 1) for i in range(1, tiles -...  4.33 us
    ppermute x1, waiting for transfers between devices, body(): inner = lax.ppermute(wide, 'ry', [(i, i ^ 1) for i in range(bands)])  2.72 us
    pallas_call x1, Pallas kernels, body(): call(lon_kernel, [struct((ROWS, 2 * CX), F32), struct((2 * CX, CX), BF16)...  2.48 us
    ppermute x1, starting transfers between devices, body(): lax.ppermute(wide, 'ry', [(i, (i + 1 ^ 1) - 1) for i in range(1, bands -...  2.17 us
    pallas_call x1, Pallas kernels, body(): call(pack_kernel, struct((TILES, 4 * PARTS, CX), BF16), [pl.BlockSpec(mem...  1.96 us
  transfers between devices with their start and end apart: 5, of which 3 were waited for; matrix products, arithmetic and copies ran while one was open for 0% of the time, Pallas kernels for 10%

profile of v5, /device:TPU:24, one launch (start us, length us, event | category | flops | bytes accessed | tf_op | source)
XLA Modules:
  0.0 38.0 jit_solution(10542270106137022348)
XLA Ops:
  0.7 0.0 copy-start
  0.7 0.0 copy-start.3
  0.7 2.0 %shard_map.91 = bf16[16,32,128]{2,1,0:T(8,128)(2,1)} custom-call(s32[1]{0:T(128)S(6)} %copy.10.count_ref, s32[8,128]{1,0:T(8,128)} %bitcast.22, s32[8,128]{1,0:T(8,128)} %bitcast.23, f32[2,1024]{1,0:T(2,128)} %value_hbm.1), custom_call_target="tpu_custom_call" | custom-call | flops 3000000000 | bytes 200000 | tf_op jit(solution)/shard_map/pallas_call | solution.py:221
  2.6 5.8 %all-to-all-start = ((bf16[16,32,128]{2,1,0:T(8,128)(2,1)}), bf16[16,32,128]{2,1,0:T(8,128)(2,1)S(1)}, u32[]{:S(2)}, u32[]{:S(2)}) async-start(bf16[16,32,128]{2,1,0:T(8,128)(2,1)} %shard_map.91), calls=%async_computation | async-start | bytes 262144 | tf_op jit(solution)/shard_map/all_to_all | solution.py:234
  8.4 0.0 copy-done
  8.4 4.3 %collective-permute-start.1 = (bf16[2,64,8,128]{3,2,1,0:T(8,128)(2,1)S(1)}, bf16[2,64,8,128]{3,2,1,0:T(8,128)(2,1)S(1)}, u32[]{:S(2)}, u32[]{:S(2)}) collective-permute-start(bf16[2,64,8,128]{3,2,1,0:T(8,128)(2,1)S(1)} %copy-done), channel_id=1, source_target_pairs={{1,2},{2,1},{3,4},{4,3},{5,6},{6,5},{7,8},{8,7},{9,10},{10,9},{11,... | collective-permute-start | bytes 786440 | tf_op jit(solution)/shard_map/ppermute | solution.py:238
  12.8 1.9 %collective-permute-start = (bf16[2,64,8,128]{3,2,1,0:T(8,128)(2,1)S(1)}, bf16[2,64,8,128]{3,2,1,0:T(8,128)(2,1)S(1)}, u32[]{:S(2)}, u32[]{:S(2)}) collective-permute-start(bf16[2,64,8,128]{3,2,1,0:T(8,128)(2,1)S(1)} %copy-done), channel_id=1, source_target_pairs={{0,1},{1,0},{2,3},{3,2},{4,5},{5,4},{6,7},{7,6},{8,9},{9,8},{10,11... | collective-permute-start | bytes 786440 | tf_op jit(solution)/shard_map/ppermute | solution.py:237
  14.7 0.0 all-to-all-done.record_ref
  14.7 0.0 copy-done.3
  14.7 0.0 copy-start.1
  14.7 0.0 copy-start.2
  14.7 0.0 copy-start.4
  14.8 2.5 %shard_map.92 = (f32[512,256]{1,0:T(8,128)S(1)}, bf16[256,128]{1,0:T(8,128)(2,1)S(1)}) custom-call(bf16[16,32,128]{2,1,0:T(8,128)(2,1)S(1)} %all-to-all-done.record_ref, bf16[1024,128]{1,0:T(8,128)(2,1)S(1)} %bitcast.18, f32[16,128]{1,0:T(8,128)S(1)} %bitcast.20), custom_call_target="tpu_custom_call" | custom-call | flops 4294967296 | bytes 1000000 | tf_op jit(solution)/shard_map/pallas_call | solution.py:240
  17.3 1.0 %collective-permute-done.1 = bf16[2,64,8,128]{3,2,1,0:T(8,128)(2,1)S(1)} collective-permute-done((bf16[2,64,8,128]{3,2,1,0:T(8,128)(2,1)S(1)}, bf16[2,64,8,128]{3,2,1,0:T(8,128)(2,1)S(1)}, u32[]{:S(2)}, u32[]{:S(2)}) %collective-permute-start.1) | collective-permute-done | bytes 262176 | tf_op jit(solution)/shard_map/ppermute | solution.py:238
  18.2 0.0 collective-permute-done
  18.2 0.3 shard_map.93.smooth_ref
  18.5 6.5 %collective-permute-start.2 = (bf16[2,64,8,128]{3,2,1,0:T(8,128)(2,1)S(1)}, bf16[2,64,8,128]{3,2,1,0:T(8,128)(2,1)S(1)}, u32[]{:S(2)}, u32[]{:S(2)}) collective-permute-start(bf16[2,64,8,128]{3,2,1,0:T(8,128)(2,1)S(1)} %bitcast.13), channel_id=1, source_target_pairs={{0,16},{16,0},{32,48},{48,32},{64,80},{80,64},{96,112},{112,96},{1... | collective-permute-start | bytes 786440 | tf_op jit(solution)/shard_map/ppermute | solution.py:259
  25.1 2.2 %collective-permute-start.3 = (bf16[2,64,8,128]{3,2,1,0:T(8,128)(2,1)S(1)}, bf16[2,64,8,128]{3,2,1,0:T(8,128)(2,1)S(1)}, u32[]{:S(2)}, u32[]{:S(2)}) collective-permute-start(bf16[2,64,8,128]{3,2,1,0:T(8,128)(2,1)S(1)} %bitcast.14), channel_id=1, source_target_pairs={{16,32},{32,16},{48,64},{64,48},{80,96},{96,80},{112,128},{128,112... | collective-permute-start | bytes 786440 | tf_op jit(solution)/shard_map/ppermute | solution.py:260
  27.2 0.0 copy-done.1
  27.3 0.0 copy-done.2
  27.3 0.0 copy-done.4
  27.3 1.0 %shard_map.94 = (f32[1024,128]{1,0:T(8,128)S(1)}, bf16[2,2,512,512]{3,2,1,0:T(8,128)(2,1)S(1)}) custom-call(bf16[1024,128]{1,0:T(8,128)(2,1)S(1)} %shard_map.93.smooth_ref, bf16[1024,128]{1,0:T(8,128)(2,1)S(1)} %bitcast.19, f32[1,8]{1,0:T(1,128)S(1)} %bitcast.21, bf16[2,64,64]{2,1,0:T(8,128)(2,1)S(1)} %copy-done.2), custom_call_target="tpu_custom_call" | custom-call | flops 268435456 | bytes 4000000 | tf_op jit(solution)/shard_map/pallas_call | solution.py:261
  28.3 2.7 %collective-permute-done.2 = bf16[2,64,8,128]{3,2,1,0:T(8,128)(2,1)S(1)} collective-permute-done((bf16[2,64,8,128]{3,2,1,0:T(8,128)(2,1)S(1)}, bf16[2,64,8,128]{3,2,1,0:T(8,128)(2,1)S(1)}, u32[]{:S(2)}, u32[]{:S(2)}) %collective-permute-start.2) | collective-permute-done | bytes 262176 | tf_op jit(solution)/shard_map/ppermute | solution.py:259
  31.0 0.4 %shard_map.95.total_ref = f32[1024,128]{1,0:T(8,128)S(1)} custom-call(f32[1024,128]{1,0:T(8,128)S(1)} %get-tuple-element.13.total_ref, bf16[1024,128]{1,0:T(8,128)(2,1)S(1)} %bitcast.17, bf16[2,2,512,512]{3,2,1,0:T(8,128)(2,1)S(1)} %get-tuple-element.14.y_ref), custom_call_target="tpu_custom_call" | custom-call | flops 134217728 | bytes 2000000 | tf_op jit(solution)/shard_map/pallas_call | solution.py:269
  31.5 5.3 %collective-permute-done.3 = bf16[2,64,8,128]{3,2,1,0:T(8,128)(2,1)S(1)} collective-permute-done((bf16[2,64,8,128]{3,2,1,0:T(8,128)(2,1)S(1)}, bf16[2,64,8,128]{3,2,1,0:T(8,128)(2,1)S(1)}, u32[]{:S(2)}, u32[]{:S(2)}) %collective-permute-start.3) | collective-permute-done | bytes 262176 | tf_op jit(solution)/shard_map/ppermute | solution.py:260
  36.8 1.2 %shard_map.96 = bf16[1024,128]{1,0:T(8,128)(2,1)} custom-call(f32[1024,128]{1,0:T(8,128)S(1)} %shard_map.95.total_ref, bf16[1024,128]{1,0:T(8,128)(2,1)S(1)} %bitcast.12, bf16[2,2,512,512]{3,2,1,0:T(8,128)(2,1)S(1)} %get-tuple-element.14.y_ref), custom_call_target="tpu_custom_call" | custom-call | flops 134217728 | bytes 2000000 | tf_op jit(solution)/shard_map/pallas_call | solution.py:269
Async XLA Ops:
  0.7 7.8 %copy-start = (bf16[2,64,8,128]{3,2,1,0:T(8,128)(2,1)S(1)}, bf16[2,64,8,128]{3,2,1,0:T(8,128)(2,1)}, u32[]{:S(2)}) copy-start(bf16[2,64,8,128]{3,2,1,0:T(8,128)(2,1)} %param.10) | copy-start | bytes 786436
  0.7 14.1 %copy-start.3 = (f32[2048]{0:T(1024)S(1)}, f32[2048]{0:T(1024)}, u32[]{:S(2)}) copy-start(f32[2048]{0:T(1024)} %param.15) | copy-start | bytes 24580
  2.6 12.1 %all-to-all-start = ((bf16[16,32,128]{2,1,0:T(8,128)(2,1)}), bf16[16,32,128]{2,1,0:T(8,128)(2,1)S(1)}, u32[]{:S(2)}, u32[]{:S(2)}) async-start(bf16[16,32,128]{2,1,0:T(8,128)(2,1)} %shard_map.91), calls=%async_computation | async-start | bytes 262144 | tf_op jit(solution)/shard_map/all_to_all | solution.py:234
  8.4 9.8 %collective-permute-start.1 = (bf16[2,64,8,128]{3,2,1,0:T(8,128)(2,1)S(1)}, bf16[2,64,8,128]{3,2,1,0:T(8,128)(2,1)S(1)}, u32[]{:S(2)}, u32[]{:S(2)}) collective-permute-start(bf16[2,64,8,128]{3,2,1,0:T(8,128)(2,1)S(1)} %copy-done), channel_id=1, source_target_pairs={{1,2},{2,1},{3,4},{4,3},{5,6},{6,5},{7,8},{8,7},{9,10},{10,9},{11,... | collective-permute-start | bytes 786440 | tf_op jit(solution)/shard_map/ppermute | solution.py:238
  12.8 5.5 %collective-permute-start = (bf16[2,64,8,128]{3,2,1,0:T(8,128)(2,1)S(1)}, bf16[2,64,8,128]{3,2,1,0:T(8,128)(2,1)S(1)}, u32[]{:S(2)}, u32[]{:S(2)}) collective-permute-start(bf16[2,64,8,128]{3,2,1,0:T(8,128)(2,1)S(1)} %copy-done), channel_id=1, source_target_pairs={{0,1},{1,0},{2,3},{3,2},{4,5},{5,4},{6,7},{7,6},{8,9},{9,8},{10,11... | collective-permute-start | bytes 786440 | tf_op jit(solution)/shard_map/ppermute | solution.py:237
  14.7 12.5 %copy-start.1 = (bf16[2,64,8,128]{3,2,1,0:T(8,128)(2,1)S(1)}, bf16[2,64,8,128]{3,2,1,0:T(8,128)(2,1)}, u32[]{:S(2)}) copy-start(bf16[2,64,8,128]{3,2,1,0:T(8,128)(2,1)} %param.9) | copy-start | bytes 786436
  14.7 12.5 %copy-start.2 = (bf16[2,64,64]{2,1,0:T(8,128)(2,1)S(1)}, bf16[2,64,64]{2,1,0:T(8,128)(2,1)}, u32[]{:S(2)}) copy-start(bf16[2,64,64]{2,1,0:T(8,128)(2,1)} %vert_ref.1) | copy-start | bytes 49156
  14.7 12.5 %copy-start.4 = (f32[8]{0:T(128)S(1)}, f32[8]{0:T(128)}, u32[]{:S(2)}) copy-start(f32[8]{0:T(128)} %param.16) | copy-start | bytes 100
  18.5 12.5 %collective-permute-start.2 = (bf16[2,64,8,128]{3,2,1,0:T(8,128)(2,1)S(1)}, bf16[2,64,8,128]{3,2,1,0:T(8,128)(2,1)S(1)}, u32[]{:S(2)}, u32[]{:S(2)}) collective-permute-start(bf16[2,64,8,128]{3,2,1,0:T(8,128)(2,1)S(1)} %bitcast.13), channel_id=1, source_target_pairs={{0,16},{16,0},{32,48},{48,32},{64,80},{80,64},{96,112},{112,96},{1... | collective-permute-start | bytes 786440 | tf_op jit(solution)/shard_map/ppermute | solution.py:259
  25.1 11.7 %collective-permute-start.3 = (bf16[2,64,8,128]{3,2,1,0:T(8,128)(2,1)S(1)}, bf16[2,64,8,128]{3,2,1,0:T(8,128)(2,1)S(1)}, u32[]{:S(2)}, u32[]{:S(2)}) collective-permute-start(bf16[2,64,8,128]{3,2,1,0:T(8,128)(2,1)S(1)} %bitcast.14), channel_id=1, source_target_pairs={{16,32},{32,16},{48,64},{64,48},{80,96},{96,80},{112,128},{128,112... | collective-permute-start | bytes 786440 | tf_op jit(solution)/shard_map/ppermute | solution.py:260

commit v6 on v5

--- a/solution.py
+++ b/solution.py
@@ -88,19 +88,28 @@
     field = lambda f: record[:, f * PARTS : (f + 1) * PARTS, :].reshape(rows, CX)
     column = field(1)
     reached = jnp.logical_and(column >= -1.5 * CX, column < 1.5 * CX)
-    some = jnp.max(jnp.where(reached, 1.0, 0.0), axis=1, keepdims=True)
-    some = jnp.broadcast_to(some, (rows, CX)).astype(BF16)
-    across = (((0,), (0,)), ((), ()))
-    upto = (iota((rows, rows), 0) <= iota((rows, rows), 1)).astype(F32).astype(BF16)
-    under = (iota((rows, rows), 0) < iota((rows, rows), 1)).astype(F32).astype(BF16)
-    upto = lax.dot_general(some, upto, across, preferred_element_type=F32)
-    under = lax.dot_general(some, under, across, preferred_element_type=F32)
-    target_row = iota((rows, rows), 0).astype(F32)
-    moved = jnp.logical_and(under == target_row, upto == target_row + 1.0)
-    moved = jnp.where(moved, 1.0, 0.0).astype(BF16)
+    count = jnp.sum(jnp.where(reached, 1.0, 0.0), axis=1, keepdims=True)
+    count = jnp.broadcast_to(count, (rows, CX))
+    some = jnp.where(count > 0.0, 1.0, 0.0).astype(BF16)
+    count = count.astype(BF16)
+    row, other = iota((rows, rows), 0), iota((rows, rows), 1)
+    source = row // PARTS == other // PARTS
+    matrix = lambda mask: mask.astype(F32).astype(BF16)
+    turned = lambda x, mask: lax.dot_general(x, matrix(mask), (((0,), (0,)), ((), ())), preferred_element_type=F32)
+    flag = turned(some, row == other)
+    following = turned(some, jnp.logical_and(row == other + 1, source))
+    span = turned(some, source)
+    within = turned(count, source)
+    fits = jnp.logical_and(span > 1.0, within <= CX * (span - 1.0))
+    merged = jnp.where(fits, flag * (1.0 - following), 0.0)
+    kept = flag - merged
+    ahead = jnp.dot(kept.astype(BF16), matrix(row < other), preferred_element_type=F32)
+    place = ahead - merged * (span - 1.0)
+    moved = matrix(jnp.logical_and(flag > 0.0, place == row.astype(F32)))
     for f in range(4):
-        list_ref[f] = jnp.dot(moved, field(f).astype(BF16), preferred_element_type=F32)
-    used_rows = jnp.max(upto).astype(I32)
+        kept_slots = jnp.where(reached, field(f), 0.0).astype(BF16)
+        list_ref[f] = jnp.dot(moved, kept_slots, preferred_element_type=F32)
+    used_rows = jnp.max(ahead + kept).astype(I32)
 
     tile, tiles = lax.axis_index("rx"), lax.axis_size("rx")
     copies[0].wait()

time: 38.7 us -> 38.5 us (level)
  transfers between devices with their start and end apart: 5 -> 5, of which waited for: 3 -> 3; matrix products, arithmetic and copies ran while one was open for 0% -> 0% of each run, Pallas kernels for 10% -> 11%
where the time goes in v6:
time: 38.5 us; the launch traced here: 38.1 us
  starting transfers between devices  20.8 us (54%)
  waiting for transfers between devices  9.05 us (24%)
  Pallas kernels  7.49 us (19%)
  between operations  0.8 us (2%)
    ppermute x1, starting transfers between devices, body(): inner = lax.ppermute(wide, 'ry', [(i, i ^ 1) for i in range(bands)])  6.54 us
    all_to_all x1, starting transfers between devices, body(): records = lax.all_to_all(packed, 'rx', 0, 0, tiled=True)  5.79 us
    ppermute x1, waiting for transfers between devices, body(): lax.ppermute(wide, 'ry', [(i, (i + 1 ^ 1) - 1) for i in range(1, bands -...  5.33 us
    ppermute x1, starting transfers between devices, body(): lax.ppermute(held, 'rx', [(i, (i + 1 ^ 1) - 1) for i in range(1, tiles -...  4.33 us
    ppermute x1, waiting for transfers between devices, body(): inner = lax.ppermute(wide, 'ry', [(i, i ^ 1) for i in range(bands)])  2.88 us
    pallas_call x1, Pallas kernels, body(): call(lon_kernel, [struct((ROWS, 2 * CX), F32), struct((2 * CX, CX), BF16)...  2.64 us
    ppermute x1, starting transfers between devices, body(): lax.ppermute(wide, 'ry', [(i, (i + 1 ^ 1) - 1) for i in range(1, bands -...  2.17 us
    pallas_call x1, Pallas kernels, body(): call(pack_kernel, struct((TILES, 4 * PARTS, CX), BF16), [pl.BlockSpec(mem...  1.96 us
  transfers between devices with their start and end apart: 5, of which 3 were waited for; matrix products, arithmetic and copies ran while one was open for 0% of the time, Pallas kernels for 11%

profile of v6, /device:TPU:24, one launch (start us, length us, event | category | flops | bytes accessed | tf_op | source)
XLA Modules:
  0.0 38.1 jit_solution(12111451297584186474)
XLA Ops:
  0.7 0.0 copy-start
  0.7 0.0 copy-start.3
  0.7 2.0 %shard_map.91 = bf16[16,32,128]{2,1,0:T(8,128)(2,1)} custom-call(s32[1]{0:T(128)S(6)} %copy.10.count_ref, s32[8,128]{1,0:T(8,128)} %bitcast.22, s32[8,128]{1,0:T(8,128)} %bitcast.23, f32[2,1024]{1,0:T(2,128)} %value_hbm.1), custom_call_target="tpu_custom_call" | custom-call | flops 3000000000 | bytes 200000 | tf_op jit(solution)/shard_map/pallas_call | solution.py:230
  2.6 5.8 %all-to-all-start = ((bf16[16,32,128]{2,1,0:T(8,128)(2,1)}), bf16[16,32,128]{2,1,0:T(8,128)(2,1)S(1)}, u32[]{:S(2)}, u32[]{:S(2)}) async-start(bf16[16,32,128]{2,1,0:T(8,128)(2,1)} %shard_map.91), calls=%async_computation | async-start | bytes 262144 | tf_op jit(solution)/shard_map/all_to_all | solution.py:243
  8.4 0.0 copy-done
  8.4 4.3 %collective-permute-start.1 = (bf16[2,64,8,128]{3,2,1,0:T(8,128)(2,1)S(1)}, bf16[2,64,8,128]{3,2,1,0:T(8,128)(2,1)S(1)}, u32[]{:S(2)}, u32[]{:S(2)}) collective-permute-start(bf16[2,64,8,128]{3,2,1,0:T(8,128)(2,1)S(1)} %copy-done), channel_id=1, source_target_pairs={{1,2},{2,1},{3,4},{4,3},{5,6},{6,5},{7,8},{8,7},{9,10},{10,9},{11,... | collective-permute-start | bytes 786440 | tf_op jit(solution)/shard_map/ppermute | solution.py:247
  12.8 1.9 %collective-permute-start = (bf16[2,64,8,128]{3,2,1,0:T(8,128)(2,1)S(1)}, bf16[2,64,8,128]{3,2,1,0:T(8,128)(2,1)S(1)}, u32[]{:S(2)}, u32[]{:S(2)}) collective-permute-start(bf16[2,64,8,128]{3,2,1,0:T(8,128)(2,1)S(1)} %copy-done), channel_id=1, source_target_pairs={{0,1},{1,0},{2,3},{3,2},{4,5},{5,4},{6,7},{7,6},{8,9},{9,8},{10,11... | collective-permute-start | bytes 786440 | tf_op jit(solution)/shard_map/ppermute | solution.py:246
  14.7 0.0 all-to-all-done.record_ref
  14.7 0.0 copy-done.3
  14.7 0.0 copy-start.1
  14.7 0.0 copy-start.2
  14.7 0.0 copy-start.4
  14.8 2.6 %shard_map.92 = (f32[512,256]{1,0:T(8,128)S(1)}, bf16[256,128]{1,0:T(8,128)(2,1)S(1)}) custom-call(bf16[16,32,128]{2,1,0:T(8,128)(2,1)S(1)} %all-to-all-done.record_ref, bf16[1024,128]{1,0:T(8,128)(2,1)S(1)} %bitcast.18, f32[16,128]{1,0:T(8,128)S(1)} %bitcast.20), custom_call_target="tpu_custom_call" | custom-call | flops 4294967296 | bytes 1000000 | tf_op jit(solution)/shard_map/pallas_call | solution.py:249
  17.4 0.8 %collective-permute-done.1 = bf16[2,64,8,128]{3,2,1,0:T(8,128)(2,1)S(1)} collective-permute-done((bf16[2,64,8,128]{3,2,1,0:T(8,128)(2,1)S(1)}, bf16[2,64,8,128]{3,2,1,0:T(8,128)(2,1)S(1)}, u32[]{:S(2)}, u32[]{:S(2)}) %collective-permute-start.1) | collective-permute-done | bytes 262176 | tf_op jit(solution)/shard_map/ppermute | solution.py:247
  18.2 0.0 collective-permute-done
  18.2 0.3 shard_map.93.smooth_ref
  18.5 6.5 %collective-permute-start.2 = (bf16[2,64,8,128]{3,2,1,0:T(8,128)(2,1)S(1)}, bf16[2,64,8,128]{3,2,1,0:T(8,128)(2,1)S(1)}, u32[]{:S(2)}, u32[]{:S(2)}) collective-permute-start(bf16[2,64,8,128]{3,2,1,0:T(8,128)(2,1)S(1)} %bitcast.13), channel_id=1, source_target_pairs={{0,16},{16,0},{32,48},{48,32},{64,80},{80,64},{96,112},{112,96},{1... | collective-permute-start | bytes 786440 | tf_op jit(solution)/shard_map/ppermute | solution.py:268
  25.1 2.2 %collective-permute-start.3 = (bf16[2,64,8,128]{3,2,1,0:T(8,128)(2,1)S(1)}, bf16[2,64,8,128]{3,2,1,0:T(8,128)(2,1)S(1)}, u32[]{:S(2)}, u32[]{:S(2)}) collective-permute-start(bf16[2,64,8,128]{3,2,1,0:T(8,128)(2,1)S(1)} %bitcast.14), channel_id=1, source_target_pairs={{16,32},{32,16},{48,64},{64,48},{80,96},{96,80},{112,128},{128,112... | collective-permute-start | bytes 786440 | tf_op jit(solution)/shard_map/ppermute | solution.py:269
  27.2 0.0 copy-done.1
  27.3 0.0 copy-done.2
  27.3 0.0 copy-done.4
  27.3 1.0 %shard_map.94 = (f32[1024,128]{1,0:T(8,128)S(1)}, bf16[2,2,512,512]{3,2,1,0:T(8,128)(2,1)S(1)}) custom-call(bf16[1024,128]{1,0:T(8,128)(2,1)S(1)} %shard_map.93.smooth_ref, bf16[1024,128]{1,0:T(8,128)(2,1)S(1)} %bitcast.19, f32[1,8]{1,0:T(1,128)S(1)} %bitcast.21, bf16[2,64,64]{2,1,0:T(8,128)(2,1)S(1)} %copy-done.2), custom_call_target="tpu_custom_call" | custom-call | flops 268435456 | bytes 4000000 | tf_op jit(solution)/shard_map/pallas_call | solution.py:270
  28.3 2.9 %collective-permute-done.2 = bf16[2,64,8,128]{3,2,1,0:T(8,128)(2,1)S(1)} collective-permute-done((bf16[2,64,8,128]{3,2,1,0:T(8,128)(2,1)S(1)}, bf16[2,64,8,128]{3,2,1,0:T(8,128)(2,1)S(1)}, u32[]{:S(2)}, u32[]{:S(2)}) %collective-permute-start.2) | collective-permute-done | bytes 262176 | tf_op jit(solution)/shard_map/ppermute | solution.py:268
  31.2 0.4 %shard_map.95.total_ref = f32[1024,128]{1,0:T(8,128)S(1)} custom-call(f32[1024,128]{1,0:T(8,128)S(1)} %get-tuple-element.13.total_ref, bf16[1024,128]{1,0:T(8,128)(2,1)S(1)} %bitcast.17, bf16[2,2,512,512]{3,2,1,0:T(8,128)(2,1)S(1)} %get-tuple-element.14.y_ref), custom_call_target="tpu_custom_call" | custom-call | flops 134217728 | bytes 2000000 | tf_op jit(solution)/shard_map/pallas_call | solution.py:278
  31.6 5.3 %collective-permute-done.3 = bf16[2,64,8,128]{3,2,1,0:T(8,128)(2,1)S(1)} collective-permute-done((bf16[2,64,8,128]{3,2,1,0:T(8,128)(2,1)S(1)}, bf16[2,64,8,128]{3,2,1,0:T(8,128)(2,1)S(1)}, u32[]{:S(2)}, u32[]{:S(2)}) %collective-permute-start.3) | collective-permute-done | bytes 262176 | tf_op jit(solution)/shard_map/ppermute | solution.py:269
  37.0 1.2 %shard_map.96 = bf16[1024,128]{1,0:T(8,128)(2,1)} custom-call(f32[1024,128]{1,0:T(8,128)S(1)} %shard_map.95.total_ref, bf16[1024,128]{1,0:T(8,128)(2,1)S(1)} %bitcast.12, bf16[2,2,512,512]{3,2,1,0:T(8,128)(2,1)S(1)} %get-tuple-element.14.y_ref), custom_call_target="tpu_custom_call" | custom-call | flops 134217728 | bytes 2000000 | tf_op jit(solution)/shard_map/pallas_call | solution.py:278
Async XLA Ops:
  0.7 7.8 %copy-start = (bf16[2,64,8,128]{3,2,1,0:T(8,128)(2,1)S(1)}, bf16[2,64,8,128]{3,2,1,0:T(8,128)(2,1)}, u32[]{:S(2)}) copy-start(bf16[2,64,8,128]{3,2,1,0:T(8,128)(2,1)} %param.10) | copy-start | bytes 786436
  0.7 14.1 %copy-start.3 = (f32[2048]{0:T(1024)S(1)}, f32[2048]{0:T(1024)}, u32[]{:S(2)}) copy-start(f32[2048]{0:T(1024)} %param.15) | copy-start | bytes 24580
  2.6 12.1 %all-to-all-start = ((bf16[16,32,128]{2,1,0:T(8,128)(2,1)}), bf16[16,32,128]{2,1,0:T(8,128)(2,1)S(1)}, u32[]{:S(2)}, u32[]{:S(2)}) async-start(bf16[16,32,128]{2,1,0:T(8,128)(2,1)} %shard_map.91), calls=%async_computation | async-start | bytes 262144 | tf_op jit(solution)/shard_map/all_to_all | solution.py:243
  8.4 9.8 %collective-permute-start.1 = (bf16[2,64,8,128]{3,2,1,0:T(8,128)(2,1)S(1)}, bf16[2,64,8,128]{3,2,1,0:T(8,128)(2,1)S(1)}, u32[]{:S(2)}, u32[]{:S(2)}) collective-permute-start(bf16[2,64,8,128]{3,2,1,0:T(8,128)(2,1)S(1)} %copy-done), channel_id=1, source_target_pairs={{1,2},{2,1},{3,4},{4,3},{5,6},{6,5},{7,8},{8,7},{9,10},{10,9},{11,... | collective-permute-start | bytes 786440 | tf_op jit(solution)/shard_map/ppermute | solution.py:247
  12.8 5.5 %collective-permute-start = (bf16[2,64,8,128]{3,2,1,0:T(8,128)(2,1)S(1)}, bf16[2,64,8,128]{3,2,1,0:T(8,128)(2,1)S(1)}, u32[]{:S(2)}, u32[]{:S(2)}) collective-permute-start(bf16[2,64,8,128]{3,2,1,0:T(8,128)(2,1)S(1)} %copy-done), channel_id=1, source_target_pairs={{0,1},{1,0},{2,3},{3,2},{4,5},{5,4},{6,7},{7,6},{8,9},{9,8},{10,11... | collective-permute-start | bytes 786440 | tf_op jit(solution)/shard_map/ppermute | solution.py:246
  14.7 12.5 %copy-start.1 = (bf16[2,64,8,128]{3,2,1,0:T(8,128)(2,1)S(1)}, bf16[2,64,8,128]{3,2,1,0:T(8,128)(2,1)}, u32[]{:S(2)}) copy-start(bf16[2,64,8,128]{3,2,1,0:T(8,128)(2,1)} %param.9) | copy-start | bytes 786436
  14.7 12.5 %copy-start.2 = (bf16[2,64,64]{2,1,0:T(8,128)(2,1)S(1)}, bf16[2,64,64]{2,1,0:T(8,128)(2,1)}, u32[]{:S(2)}) copy-start(bf16[2,64,64]{2,1,0:T(8,128)(2,1)} %vert_ref.1) | copy-start | bytes 49156
  14.7 12.5 %copy-start.4 = (f32[8]{0:T(128)S(1)}, f32[8]{0:T(128)}, u32[]{:S(2)}) copy-start(f32[8]{0:T(128)} %param.16) | copy-start | bytes 100
  18.5 12.7 %collective-permute-start.2 = (bf16[2,64,8,128]{3,2,1,0:T(8,128)(2,1)S(1)}, bf16[2,64,8,128]{3,2,1,0:T(8,128)(2,1)S(1)}, u32[]{:S(2)}, u32[]{:S(2)}) collective-permute-start(bf16[2,64,8,128]{3,2,1,0:T(8,128)(2,1)S(1)} %bitcast.13), channel_id=1, source_target_pairs={{0,16},{16,0},{32,48},{48,32},{64,80},{80,64},{96,112},{112,96},{1... | collective-permute-start | bytes 786440 | tf_op jit(solution)/shard_map/ppermute | solution.py:268
  25.1 11.9 %collective-permute-start.3 = (bf16[2,64,8,128]{3,2,1,0:T(8,128)(2,1)S(1)}, bf16[2,64,8,128]{3,2,1,0:T(8,128)(2,1)S(1)}, u32[]{:S(2)}, u32[]{:S(2)}) collective-permute-start(bf16[2,64,8,128]{3,2,1,0:T(8,128)(2,1)S(1)} %bitcast.14), channel_id=1, source_target_pairs={{16,32},{32,16},{48,64},{64,48},{80,96},{96,80},{112,128},{128,112... | collective-permute-start | bytes 786440 | tf_op jit(solution)/shard_map/ppermute | solution.py:269
